TPU v7x, 256 devices: a whole 4x4x8 slice. The times are simulated.
256 devices in a mesh: grp: 8 (over y, core), ctx: 32 (over z, x).
Axes of the slice: x: 4, y: 4, z: 8, core: 2. Of those that a mesh axis runs over, the one named last changes fastest.
Arguments:
- queries: bfloat16 [512, 8192], P(('grp', 'ctx')), parts along dimension 0, may hold values from -12 to 12
- prefix_keys: bfloat16 [524288, 1024], P(('grp', 'ctx')), parts along dimension 0, may hold values from -8 to 8
- prefix_values: bfloat16 [524288, 1024], P(('grp', 'ctx')), parts along dimension 0, may hold values from -6 to 6
- suffix_keys: bfloat16 [512, 256, 1024], P(('grp', 'ctx')), parts along dimension 0, may hold values from -8 to 8
- suffix_values: bfloat16 [512, 256, 1024], P(('grp', 'ctx')), parts along dimension 0, may hold values from -6 to 6
- suffix_len: int32 [512], P(('grp', 'ctx')), parts along dimension 0, may hold values from 1 to 256, as said below
Outputs:
- attended: bfloat16 [512, 8192], P(('grp', 'ctx')), parts along dimension 0
There are 8 independent parts, one for each index of `grp`. A program takes and returns all parts, laid end to end along the dimension named above; each array names one. Nothing has to cross between parts.
Inputs may be any that keep to these rules, and one draw needn't show every extreme that they name: `suffix_len`: some continuation has exactly 256 valid positions.
All inputs are finite; a program needn't handle non-finite values.
Results may differ from a plain program's by a relative error of at most 0.0055.
Values may be sent and summed in bfloat16 or wider, within the bound.
No kernel may reach another device: no remote copies, remote signals or barrier semaphores. Data moves between devices by JAX's collectives and lax.ppermute only.
A program may use at most 256 MiB of HBM per device.

v0:
```python
import jax
import jax.numpy as jnp
from jax import lax
from jax.sharding import PartitionSpec as P

HD = 128


NEG_FILL = -1e30


def prefix_block(queries, key_block, value_block):
    samples = queries.shape[0]
    kv_heads = key_block.shape[1] // HD
    group = queries.shape[1] // HD // kv_heads
    length = key_block.shape[0]
    query_heads = queries.reshape(samples, kv_heads, group, HD)
    key_heads = key_block.reshape(length, kv_heads, HD)
    value_heads = value_block.reshape(length, kv_heads, HD)
    scores = jnp.einsum(
        "sgjd,cgd->sgjc", query_heads, key_heads, preferred_element_type=jnp.float32
    ) * HD ** (-0.5)
    block_max = jnp.max(scores, axis=3)
    weights = jnp.exp(scores - block_max[..., None]).astype(jnp.bfloat16)
    block_sum = jnp.sum(weights.astype(jnp.float32), axis=3)
    block_out = jnp.einsum(
        "sgjc,cgd->sgjd", weights, value_heads, preferred_element_type=jnp.float32
    )
    return (
        block_max.reshape(samples, -1),
        block_sum.reshape(samples, -1),
        block_out.reshape(samples, -1),
    )


def suffix_block(queries, suffix_keys, suffix_values, suffix_len):
    samples = suffix_keys.shape[0]
    length = suffix_keys.shape[1]
    kv_heads = suffix_keys.shape[2] // HD
    group = queries.shape[1] // HD // kv_heads
    query_heads = queries.reshape(samples, kv_heads, group, HD)
    key_heads = suffix_keys.reshape(samples, length, kv_heads, HD)
    value_heads = suffix_values.reshape(samples, length, kv_heads, HD)
    scores = jnp.einsum(
        "sgjd,stgd->sgjt", query_heads, key_heads, preferred_element_type=jnp.float32
    ) * HD ** (-0.5)
    valid = jnp.arange(length, dtype=jnp.int32)[None, :] < suffix_len[:, None]
    valid = valid[:, None, None, :]
    block_max = jnp.max(jnp.where(valid, scores, NEG_FILL), axis=3)
    weights = jnp.where(valid, jnp.exp(scores - block_max[..., None]), 0.0).astype(jnp.bfloat16)
    block_sum = jnp.sum(weights.astype(jnp.float32), axis=3)
    block_out = jnp.einsum(
        "sgjt,stgd->sgjd", weights, value_heads, preferred_element_type=jnp.float32
    )
    return (
        block_max.reshape(samples, -1),
        block_sum.reshape(samples, -1),
        block_out.reshape(samples, -1),
    )


def scale_heads(field, factor):
    dims = field.shape
    heads = factor.shape[-1]
    return (field.reshape(dims[:-1] + (heads, -1)) * factor[..., None]).reshape(dims)


def divide_heads(field, totals):
    dims = field.shape
    heads = totals.shape[-1]
    return (field.reshape(dims[:-1] + (heads, -1)) / totals[..., None]).reshape(dims)


def local(queries, prefix_keys, prefix_values, suffix_keys, suffix_values, suffix_len):
    owned = queries.shape[0]
    position = lax.axis_index("ctx") * owned
    gathered = lax.all_gather(queries, "ctx", axis=0, tiled=True)
    pre_max, pre_sum, pre_out = prefix_block(gathered, prefix_keys, prefix_values)
    suf_max, suf_sum, suf_out = suffix_block(queries, suffix_keys, suffix_values, suffix_len)
    own_rows = lax.dynamic_slice_in_dim(pre_max, position, owned, 0)
    candidate = lax.dynamic_update_slice_in_dim(
        pre_max, jnp.maximum(own_rows, suf_max), position, 0
    )
    row_top = lax.pmax(candidate, "ctx")
    pre_factor = jnp.exp(pre_max - row_top)
    total_sum, total_out = (
        lax.psum_scatter(pre_sum * pre_factor, "ctx", scatter_dimension=0, tiled=True),
        lax.psum_scatter(scale_heads(pre_out, pre_factor), "ctx", scatter_dimension=0, tiled=True),
    )
    owned_top = lax.dynamic_slice_in_dim(row_top, position, owned, 0)
    suf_factor = jnp.exp(suf_max - owned_top)
    total_sum = total_sum + suf_sum * suf_factor
    total_out = total_out + scale_heads(suf_out, suf_factor)
    return divide_heads(total_out, total_sum).astype(jnp.bfloat16)


def solution(mesh):
    placed = (
        P(("grp", "ctx"), None),
        P(("grp", "ctx"), None),
        P(("grp", "ctx"), None),
        P(("grp", "ctx"), None, None),
        P(("grp", "ctx"), None, None),
        P(("grp", "ctx")),
    )
    return jax.shard_map(
        local, mesh=mesh, in_specs=placed, out_specs=P(("grp", "ctx"), None), check_vma=False
    )
```

profile of v0, /device:TPU:22, one launch (start us, length us, event | category | flops | bytes accessed | tf_op | source)
XLA Modules:
  0.0 443.0 jit_solution(2790862660729172249)
XLA Ops:
  6.5 0.7 all-gather.3.cloned.1.call-update
  7.3 5.3 %copy.60 = bf16[256,8,8,128]{3,2,1,0:T(8,128)(2,1)} copy(bf16[256,8,8,128]{3,1,2,0:T(8,128)(2,1)} %bitcast.84) | data formatting | bytes 8388608
  12.7 0.5 select_reduce_fusion
  13.2 0.1 reshape.67
  13.3 5.2 %copy.61 = bf16[256,8,8,128]{3,2,1,0:T(8,128)(2,1)} copy(bf16[256,8,8,128]{3,1,2,0:T(8,128)(2,1)} %bitcast.85) | data formatting | bytes 8388608
  18.5 69.4 %all-gather.3.cloned.1.call-done = bf16[32,2,8192]{2,1,0:T(2,128)(2,1)} async-done(((bf16[1,2,8192]{2,1,0:T(2,128)(2,1)}), bf16[32,2,8192]{2,1,0:T(2,128)(2,1)}) %all-gather.3.cloned.1.call-update) | async-done | bytes 1048592 | tf_op jit(solution)/shard_map/all_gather | solution.py:77
  87.9 1.8 reshape.62
  89.8 16.3 %bitcast_reduce_fusion = (f32[64,8,8]{0,2,1:T(8,128)S(1)}, f32[8,2048,64,8]{1,2,3,0:T(8,128)}) fusion(bf16[64,8,8,128]{3,2,1,0:T(8,128)(2,1)S(1)} %reshape.62, bf16[2048,8,128,1]{2,1,0,3:T(8,128)(2,1)} %bitcast.81), kind=kOutput, calls=%fused_computation.1 | convolution fusion | flops 2164256768 | bytes 38813696 | tf_op jit(solution)/shard_map/sgjd,cgd->sgjc/dot_general | solution.py:20
  106.1 14.0 %convert_reduce_fusion = f32[64,8,8]{0,2,1:T(8,128)S(1)} fusion(f32[64,8,8]{0,2,1:T(8,128)S(1)} %get-tuple-element.9, f32[8,2048,64,8]{1,2,3,0:T(8,128)} %get-tuple-element.10), kind=kLoop, calls=%fused_computation.4 | loop fusion | flops 41938944 | bytes 33587200 | tf_op jit(solution)/shard_map/reduce_sum | solution.py:25
  120.2 0.1 copy.45
  120.3 132.4 %pmax.7 = f32[64,64]{1,0:T(8,128)S(1)} all-reduce(f32[64,64]{1,0:T(8,128)S(1)} %maximum_dynamic-update-slice_fusion), channel_id=1, replica_groups=mesh['grp'=8,'ctx'=32] {'ctx'}, use_global_device_ids=true, to_apply=%region_2.3 | all-reduce | flops 4096 | bytes 32768 | tf_op jit(solution)/shard_map/pmax | solution.py:84
  252.8 16.3 %fusion.7 = f32[64,8,8,128]{3,0,2,1:T(8,128)S(1)} fusion(bf16[2048,8,128,1]{2,1,0,3:T(8,128)(2,1)} %bitcast.86, f32[8,2048,64,8]{1,2,3,0:T(8,128)} %get-tuple-element.10, f32[64,8,8]{0,2,1:T(8,128)S(1)} %get-tuple-element.9), kind=kOutput, calls=%fused_computation.10 | convolution fusion | flops 2172649472 | bytes 39862272 | tf_op jit(solution)/shard_map/sgjc,cgd->sgjd/dot_general | solution.py:26
  269.1 1.2 copy.41
  270.4 0.6 mul.52
  271.0 4.5 %bitcast_multiply_fusion = f32[64,8192]{1,0:T(8,128)} fusion(f32[8,8,64,128]{3,2,1,0:T(8,128)S(1)} %bitcast.83, f32[8,8,64,128]{3,2,1,0:T(8,128)S(1)} %bitcast.82), kind=kLoop, calls=%fused_computation.9 | loop fusion | flops 524288 | bytes 6291456 | tf_op jit(solution)/shard_map/mul | solution.py:65
  275.5 0.2 convert_reduce_fusion.1
  275.7 0.1 reshape.70
  275.8 0.6 dynamic-slice
  277.0 0.3 convolution_bitcast_fusion
  277.3 0.1 copy.48
  277.4 139.9 %all-reduce.1 = f32[64,64]{0,1:T(8,128)S(1)} all-reduce(f32[64,64]{0,1:T(8,128)S(1)} %copy.48), channel_id=3, replica_groups=mesh['grp'=8,'ctx'=32] {'ctx'}, use_global_device_ids=true, to_apply=%region_5.6.clone | all-reduce | flops 4096 | bytes 32768
  417.5 0.1 broadcast_bitcast_fusion
  417.6 16.9 %all-reduce.4.cloned.1.call-done = f32[64,8192]{1,0:T(8,128)} async-done(((f32[64,8192]{1,0:T(8,128)}), f32[64,8192]{1,0:T(8,128)}) %all-reduce.4.cloned.1.call-update) | async-done | bytes 2097168
  434.5 1.7 fusion.18
  (21 shorter events, 0.4 us)
Async XLA Ops:
  6.5 6.2 %copy-start = (bf16[2,256,1024]{2,1,0:T(8,128)(2,1)S(1)}, bf16[2,256,1024]{2,1,0:T(8,128)(2,1)}, u32[]{:S(2)}) copy-start(bf16[2,256,1024]{2,1,0:T(8,128)(2,1)} %param.9) | copy-start | bytes 3145732
  6.5 81.4 %all-gather.3.cloned.1.call-start = ((), (), s32[]{:S(2)}) async-start(), calls=%async_computation | async-start | bytes 1081344 | tf_op jit(solution)/shard_map/all_gather | solution.py:77
  7.3 427.2 %all-reduce.4.cloned.1.call-start = ((), (), s32[]{:S(2)}) async-start(), calls=%async_computation.1 | async-start | bytes 4194304
  7.3 5.4 %copy-start.3 = (s32[2]{0:T(128)S(1)}, s32[2]{0:T(128)}, u32[]{:S(2)}) copy-start(s32[2]{0:T(128)} %param.11) | copy-start | bytes 28
  7.3 5.4 %copy-start.2 = (bf16[2,8192]{1,0:T(2,128)(2,1)S(1)}, bf16[2,8192]{1,0:T(2,128)(2,1)}, u32[]{:S(2)}) copy-start(bf16[2,8192]{1,0:T(2,128)(2,1)} %param.6) | copy-start | bytes 98308
  271.0 4.8 %copy-start.4 = (u32[256]{0:T(256)S(1)}, u32[256]{0:T(256)}, u32[]{:S(2)}) copy-start(u32[256]{0:T(256)} %constant.25) | copy-start | bytes 3076
  271.0 6.0 %copy-start.1 = (bf16[2,256,1024]{2,1,0:T(8,128)(2,1)S(1)}, bf16[2,256,1024]{2,1,0:T(8,128)(2,1)}, u32[]{:S(2)}) copy-start(bf16[2,256,1024]{2,1,0:T(8,128)(2,1)} %param.10) | copy-start | bytes 3145732
Sparse Core Ops, SparseCore 0:
  9.9 77.9 all-gather.2
  275.6 158.8 all-reduce.3
where the time goes:
time: 446 us; the launch traced here: 443 us
  blocking collectives  272 us (61%)
  waiting for transfers between devices  87 us (20%)
  matrix products  33.4 us (7%)
  other arithmetic  20.5 us (5%)
  local copies, waits for them, and re-layouts  15.5 us (3%)
  between operations  14.2 us (3%)
    unnamed x1, blocking collectives  140 us
    pmax x1, blocking collectives, local(): row_top = lax.pmax(candidate, 'ctx')  132 us
    all_gather x1, waiting for transfers between devices, local(): gathered = lax.all_gather(queries, 'ctx', axis=0, tiled=True)  69.4 us
    unnamed x3, waiting for transfers between devices  17.6 us
    dot_general x1, matrix products, prefix_block(): jnp.einsum('sgjd,cgd->sgjc', query_heads, key_heads, preferred_element_ty...  16.3 us
    dot_general x1, matrix products, prefix_block(): jnp.einsum('sgjc,cgd->sgjd', weights, value_heads, preferred_element_type...  16.3 us
    reduce_sum x1, other arithmetic, prefix_block(): block_sum = jnp.sum(weights.astype(jnp.float32), axis=3)  14 us
    unnamed x16, local copies, waits for them, and re-layouts  11.4 us
  transfers between devices with their start and end apart: 2, of which 2 were waited for; matrix products, arithmetic and copies ran while one was open for 3% of the time, Pallas kernels for 0%

commit v1 on v0

v1 whole, which is shorter than its diff:
```python
import functools

import jax
import jax.numpy as jnp
from jax import lax
from jax.experimental import pallas as pl
from jax.experimental.pallas import tpu as pltpu
from jax.sharding import PartitionSpec as P

HD = 128
LOG2E = 1.4426950408889634
NEG_FILL = -1e30

NT = (((1,), (1,)), ((), ()))
NN = (((1,), (0,)), ((), ()))


def dot(a, b, dims):
    return lax.dot_general(a, b, dims, preferred_element_type=jnp.float32)


def to_lanes(column, head, rows):
    lane = lax.broadcasted_iota(jnp.int32, (rows, HD), 1)
    row = lax.broadcasted_iota(jnp.int32, (rows, HD), 0) % 16
    return jnp.where(lane == head * 16 + row, column, 0.0)


def prefix_kernel(factor, chunk, q_ref, k_ref, v_ref, out_ref, acc_max, acc_sum):
    head = pl.program_id(0)
    blocks = q_ref.shape[0]
    rows = blocks * 16
    keys = k_ref[...]
    values = jnp.concatenate([v_ref[...], jnp.ones_like(v_ref)], axis=1)
    for start in range(0, rows, chunk):
        part = slice(start // 16, (start + chunk) // 16)
        queries = q_ref[part].reshape(chunk, HD)
        scores = dot(queries, keys, NT)
        top = jnp.max(scores, axis=1, keepdims=True).astype(jnp.bfloat16).astype(jnp.float32)
        weights = jnp.exp2((scores - top) * factor).astype(jnp.bfloat16)
        both = dot(weights, values, NN)
        out_ref[part, head] = both[:, :HD].astype(jnp.bfloat16).reshape(chunk // 16, 16, HD)
        here = slice(start, start + chunk)
        new_max = to_lanes(top, head, chunk)
        new_sum = to_lanes(both[:, HD:], head, chunk)

        @pl.when(head == 0)
        def _():
            acc_max[here] = new_max
            acc_sum[here] = new_sum

        @pl.when(head > 0)
        def _():
            acc_max[here] += new_max
            acc_sum[here] += new_sum

    @pl.when(head == pl.num_programs(0) - 1)
    def _():
        tops = jnp.sum(acc_max[...].reshape(blocks, 16, HD), axis=1, keepdims=True)
        sums = jnp.sum(acc_sum[...].reshape(blocks, 16, HD), axis=1, keepdims=True)
        high = sums.astype(jnp.bfloat16).astype(jnp.float32)
        row = lax.broadcasted_iota(jnp.int32, (blocks, 16, HD), 1)
        stats = jnp.where(row == 0, tops, jnp.where(row == 1, high, jnp.where(row == 2, sums - high, 0.0)))
        out_ref[:, pl.num_programs(0)] = stats.astype(jnp.bfloat16)


def prefix_part(queries, keys, values, factor):
    blocks, heads = queries.shape[:2]
    length = keys.shape[0]
    rows = blocks * 16
    return pl.pallas_call(
        functools.partial(prefix_kernel, factor, min(rows, 256)),
        grid=(heads,),
        in_specs=[
            pl.BlockSpec((blocks, None, 16, HD), lambda g: (0, g, 0, 0)),
            pl.BlockSpec((length, HD), lambda g: (0, g)),
            pl.BlockSpec((length, HD), lambda g: (0, g)),
        ],
        out_specs=pl.BlockSpec((blocks, heads + 1, 16, HD), lambda g: (0, 0, 0, 0)),
        out_shape=jax.ShapeDtypeStruct((blocks, heads + 1, 16, HD), jnp.bfloat16),
        scratch_shapes=[pltpu.VMEM((rows, HD), jnp.float32)] * 2,
        compiler_params=pltpu.CompilerParams(vmem_limit_bytes=40 * 2**20),
        cost_estimate=pl.CostEstimate(
            flops=4 * rows * heads * length * HD,
            bytes_accessed=4 * length * heads * HD + 4 * rows * heads * HD,
            transcendentals=rows * heads * length,
        ),
        name="prefix_part",
    )(queries, keys, values)


def suffix_kernel(factor, len_ref, q_ref, k_ref, v_ref, out_ref, stat_ref):
    heads = q_ref.shape[0]
    length = k_ref.shape[1]
    odd = lax.broadcasted_iota(jnp.int32, (16, length), 0) % 2 == 1
    position = lax.broadcasted_iota(jnp.int32, (16, length), 1)
    valid = position < jnp.where(odd, len_ref[1], len_ref[0])
    maxima = jnp.zeros((16, HD), jnp.float32)
    sums = jnp.zeros((16, HD), jnp.float32)
    for head in range(heads):
        cols = slice(head * HD, (head + 1) * HD)
        queries = q_ref[head]
        scores = jnp.where(odd, dot(queries, k_ref[1, :, cols], NT), dot(queries, k_ref[0, :, cols], NT))
        top = jnp.max(jnp.where(valid, scores, NEG_FILL), axis=1, keepdims=True)
        weights = jnp.where(valid, jnp.exp2((scores - top) * factor), 0.0).astype(jnp.bfloat16)
        total = jnp.sum(weights.astype(jnp.float32), axis=1, keepdims=True)
        outs = jnp.where(odd[:, :HD], dot(weights, v_ref[1, :, cols], NN), dot(weights, v_ref[0, :, cols], NN))
        out_ref[head * 16:(head + 1) * 16] = outs
        maxima += to_lanes(top, head, 16)
        sums += to_lanes(total, head, 16)
    stat_ref[0:1] = jnp.sum(maxima, axis=0, keepdims=True)
    stat_ref[1:2] = jnp.sum(sums, axis=0, keepdims=True)
    stat_ref[2:] = jnp.zeros((6, HD), jnp.float32)


def suffix_part(lengths, queries, keys, values, factor):
    heads = queries.shape[0]
    vmem = pl.BlockSpec(memory_space=pltpu.VMEM)
    return pl.pallas_call(
        functools.partial(suffix_kernel, factor),
        in_specs=[pl.BlockSpec(memory_space=pltpu.SMEM), vmem, vmem, vmem],
        out_specs=[vmem, vmem],
        out_shape=[
            jax.ShapeDtypeStruct((heads * 16, HD), jnp.float32),
            jax.ShapeDtypeStruct((8, HD), jnp.float32),
        ],
        compiler_params=pltpu.CompilerParams(vmem_limit_bytes=16 * 2**20),
        name="suffix_part",
    )(lengths, queries, keys, values)


def combine_kernel(factor, got_ref, suf_ref, stat_ref, out_ref):
    blocks = got_ref.shape[0]
    heads = got_ref.shape[1] - 1
    stats = got_ref[:, heads].astype(jnp.float32)
    tops = stats[:, 0]
    sums = stats[:, 1] + stats[:, 2]
    suf_top = stat_ref[0:1]
    top = jnp.maximum(jnp.max(tops, axis=0, keepdims=True), suf_top)
    scale = jnp.exp2((tops - top) * factor)
    suf_scale = jnp.exp2((suf_top - top) * factor)
    total = jnp.sum(scale * sums, axis=0, keepdims=True) + suf_scale * stat_ref[1:2]
    shares = jnp.concatenate(
        [scale / total, suf_scale / total, jnp.zeros((HD - blocks - 1, HD), jnp.float32)], axis=0
    )
    shares = shares.T
    acc = suf_ref[...] * shares[:, blocks:blocks + 1]
    for src in range(blocks):
        block = got_ref[src, :heads].reshape(heads * 16, HD).astype(jnp.float32)
        acc += block * shares[:, src:src + 1]
    out_ref[...] = acc.astype(jnp.bfloat16)


def combine_part(got, suf_out, suf_stats, factor):
    vmem = pl.BlockSpec(memory_space=pltpu.VMEM)
    return pl.pallas_call(
        functools.partial(combine_kernel, factor),
        in_specs=[vmem, vmem, vmem],
        out_specs=vmem,
        out_shape=jax.ShapeDtypeStruct(suf_out.shape, jnp.bfloat16),
        compiler_params=pltpu.CompilerParams(vmem_limit_bytes=16 * 2**20),
        name="combine_part",
    )(got, suf_out, suf_stats)


def local(queries, prefix_keys, prefix_values, suffix_keys, suffix_values, suffix_len):
    owned, width = queries.shape
    heads = prefix_keys.shape[1] // HD
    factor = LOG2E * HD ** -0.5
    devices = lax.axis_size("ctx")
    mine = queries.reshape(owned, heads, 8, HD).transpose(1, 2, 0, 3).reshape(heads, 16, HD)
    copies = jnp.broadcast_to(mine[None], (devices,) + mine.shape)
    gathered = lax.all_to_all(copies, "ctx", 0, 0, tiled=True)
    suf_out, suf_stats = suffix_part(suffix_len, mine, suffix_keys, suffix_values, factor)
    partial = prefix_part(gathered, prefix_keys, prefix_values, factor)
    got = lax.all_to_all(partial, "ctx", 0, 0, tiled=True)
    out = combine_part(got, suf_out, suf_stats, factor)
    return out.reshape(heads * 8, owned, HD).transpose(1, 0, 2).reshape(owned, width)


def solution(mesh):
    placed = (
        P(("grp", "ctx"), None),
        P(("grp", "ctx"), None),
        P(("grp", "ctx"), None),
        P(("grp", "ctx"), None, None),
        P(("grp", "ctx"), None, None),
        P(("grp", "ctx")),
    )
    return jax.shard_map(
        local, mesh=mesh, in_specs=placed, out_specs=P(("grp", "ctx"), None), check_vma=False
    )
```

time: 446 us -> 108 us (0.24)
  blocking collectives: 272 us -> 39.4 us
  waiting for transfers between devices: 87 us -> 27.2 us
  matrix products: 33.4 us -> 0 us
  Pallas kernels: 0 us -> 30.1 us
  other arithmetic: 20.5 us -> 0 us
  between operations: 14.2 us -> 0.06 us
  local copies, waits for them, and re-layouts: 15.5 us -> 5.37 us
  starting transfers between devices: 0.04 us -> 5.56 us
    unnamed x1 -> x0, blocking collectives: 140 us -> none
    pmax x1 -> x0, blocking collectives: 132 us -> none  [local(): row_top = lax.pmax(candidate, 'ctx')]
    all_gather x1 -> x0, waiting for transfers between devices: 69.4 us -> none  [local(): gathered = lax.all_gather(queries, 'ctx', axis=0, tiled=True)]
    all_to_all x0 -> x1, blocking collectives: none -> 39.4 us  [local(): gathered = lax.all_to_all(copies, 'ctx', 0, 0, tiled=True)]
    dot_general x4 -> x0, matrix products: 33.4 us -> none  [the longest x1 16.3 us: prefix_block(): jnp.einsum('sgjd,cgd->sgjc', query_heads, key_heads, preferred_element_ty...]
    pallas_call x0 -> x3, Pallas kernels: none -> 30.1 us  [the longest x1 26 us: prefix_part(): pl.pallas_call(functools.partial(prefix_kernel, factor, min(rows, 256)),...]
    all_to_all x0 -> x1, waiting for transfers between devices: none -> 27.2 us  [local(): got = lax.all_to_all(partial, 'ctx', 0, 0, tiled=True)]
    unnamed x3 -> x0, waiting for transfers between devices: 17.6 us -> none
  transfers between devices with their start and end apart: 2 -> 1, of which waited for: 2 -> 1; matrix products, arithmetic and copies ran while one was open for 3% -> 0% of each run, Pallas kernels for 0% -> 2%
where the time goes in v1:
time: 108 us
  blocking collectives  39.4 us (36%)
  Pallas kernels  30.1 us (28%)
  waiting for transfers between devices  27.2 us (25%)
  starting transfers between devices  5.56 us (5%)
  local copies, waits for them, and re-layouts  5.37 us (5%)
    all_to_all x1, blocking collectives, local(): gathered = lax.all_to_all(copies, 'ctx', 0, 0, tiled=True)  39.4 us
    all_to_all x1, waiting for transfers between devices, local(): got = lax.all_to_all(partial, 'ctx', 0, 0, tiled=True)  27.2 us
    pallas_call x1, Pallas kernels, prefix_part(): pl.pallas_call(functools.partial(prefix_kernel, factor, min(rows, 256)),...  26 us
    all_to_all x1, starting transfers between devices, local(): got = lax.all_to_all(partial, 'ctx', 0, 0, tiled=True)  5.56 us
    unnamed x12, local copies, waits for them, and re-layouts  4.39 us
    pallas_call x1, Pallas kernels, suffix_part(): pl.pallas_call(functools.partial(suffix_kernel, factor), in_specs=[pl.Blo...  2.54 us
  transfers between devices with their start and end apart: 1, of which 1 were waited for; matrix products, arithmetic and copies ran while one was open for 0% of the time, Pallas kernels for 2%

profile of v1, /device:TPU:22, one launch (start us, length us, event | category | flops | bytes accessed | tf_op | source)
XLA Modules:
  0.0 107.7 jit_solution(5591538532103357406)
XLA Ops:
  0.0 1.0 broadcast_in_dim.8
  1.0 39.4 %all_to_all.10.q_ref = bf16[32,8,16,128]{3,2,1,0:T(8,128)(2,1)S(1)} all-to-all(bf16[32,8,16,128]{3,2,1,0:T(8,128)(2,1)S(1)} %broadcast_in_dim.8), channel_id=1, replica_groups=mesh['grp'=8,'ctx'=32] {'ctx'}, dimensions={0} | all-to-all | bytes 2097152 | tf_op jit(solution)/shard_map/all_to_all | solution.py:172
  40.4 0.0 copy-start.4
  40.4 2.2 %copy-done.4 = bf16[2048,1024]{1,0:T(8,128)(2,1)S(1)} copy-done((bf16[2048,1024]{1,0:T(8,128)(2,1)S(1)}, bf16[2048,1024]{1,0:T(8,128)(2,1)}, u32[]{:S(2)}) %copy-start.4) | copy-done | bytes 4194328
  42.6 0.0 copy-start.5
  42.6 2.2 %copy-done.5 = bf16[2048,1024]{1,0:T(8,128)(2,1)S(1)} copy-done((bf16[2048,1024]{1,0:T(8,128)(2,1)S(1)}, bf16[2048,1024]{1,0:T(8,128)(2,1)}, u32[]{:S(2)}) %copy-start.5) | copy-done | bytes 4194328
  44.8 0.0 copy-start
  44.8 0.0 copy-start.1
  44.8 0.0 copy-start.2
  44.8 0.0 copy-start.3
  44.8 26.0 %prefix_part.1 = bf16[32,9,16,128]{3,2,1,0:T(8,128)(2,1)} custom-call(bf16[32,8,16,128]{3,2,1,0:T(8,128)(2,1)S(1)} %all_to_all.10.q_ref, bf16[2048,1024]{1,0:T(8,128)(2,1)S(1)} %copy-done.4, bf16[2048,1024]{1,0:T(8,128)(2,1)S(1)} %copy-done.5), custom_call_target="tpu_custom_call" | custom-call | flops 4294967296 | bytes 10485760 | tf_op jit(solution)/shard_map/prefix_part/pallas_call | solution.py:70
  70.8 5.6 %all-to-all-start.1 = ((bf16[32,9,16,128]{3,2,1,0:T(8,128)(2,1)}), bf16[32,9,16,128]{3,2,1,0:T(8,128)(2,1)S(1)}, u32[]{:S(2)}, u32[]{:S(2)}) async-start(bf16[32,9,16,128]{3,2,1,0:T(8,128)(2,1)} %prefix_part.1), calls=%async_computation.1 | async-start | bytes 2359296 | tf_op jit(solution)/shard_map/all_to_all | solution.py:175
  76.4 0.0 copy-done
  76.4 0.0 copy-done.1
  76.4 0.0 copy-done.2
  76.4 0.0 copy-done.3
  76.4 2.5 %suffix_part.1 = (f32[128,128]{1,0:T(8,128)S(1)}, f32[8,128]{1,0:T(8,128)S(1)}) custom-call(s32[2]{0:T(128)S(1)} %copy-done.3, bf16[8,16,128]{2,1,0:T(8,128)(2,1)S(1)} %bitcast.11, bf16[2,256,1024]{2,1,0:T(8,128)(2,1)S(1)} %copy-done, bf16[2,256,1024]{2,1,0:T(8,128)(2,1)S(1)} %copy-done.1), custom_call_target="tpu_custom_call" | custom-call | tf_op jit(solution)/shard_map/suffix_part/pallas_call | solution.py:118
  79.0 27.2 %all-to-all-done.1.got_ref = bf16[32,9,16,128]{3,2,1,0:T(8,128)(2,1)S(1)} async-done(((bf16[32,9,16,128]{3,2,1,0:T(8,128)(2,1)}), bf16[32,9,16,128]{3,2,1,0:T(8,128)(2,1)S(1)}, u32[]{:S(2)}, u32[]{:S(2)}) %all-to-all-start.1) | async-done | bytes 1179680 | tf_op jit(solution)/shard_map/all_to_all | solution.py:175
  106.2 1.5 %combine_part.1 = bf16[128,128]{1,0:T(8,128)(2,1)} custom-call(bf16[32,9,16,128]{3,2,1,0:T(8,128)(2,1)S(1)} %all-to-all-done.1.got_ref, f32[128,128]{1,0:T(8,128)S(1)} %get-tuple-element.7.suf_ref, f32[8,128]{1,0:T(8,128)S(1)} %get-tuple-element.8.stat_ref), custom_call_target="tpu_custom_call" | custom-call | tf_op jit(solution)/shard_map/combine_part/pallas_call | solution.py:155
Async XLA Ops:
  40.4 2.2 %copy-start.4 = (bf16[2048,1024]{1,0:T(8,128)(2,1)S(1)}, bf16[2048,1024]{1,0:T(8,128)(2,1)}, u32[]{:S(2)}) copy-start(bf16[2048,1024]{1,0:T(8,128)(2,1)} %k_ref.2) | copy-start | bytes 12582916
  42.6 2.2 %copy-start.5 = (bf16[2048,1024]{1,0:T(8,128)(2,1)S(1)}, bf16[2048,1024]{1,0:T(8,128)(2,1)}, u32[]{:S(2)}) copy-start(bf16[2048,1024]{1,0:T(8,128)(2,1)} %v_ref.2) | copy-start | bytes 12582916
  44.8 31.6 %copy-start = (bf16[2,256,1024]{2,1,0:T(8,128)(2,1)S(1)}, bf16[2,256,1024]{2,1,0:T(8,128)(2,1)}, u32[]{:S(2)}) copy-start(bf16[2,256,1024]{2,1,0:T(8,128)(2,1)} %k_ref.3) | copy-start | bytes 3145732
  44.8 31.6 %copy-start.1 = (bf16[2,256,1024]{2,1,0:T(8,128)(2,1)S(1)}, bf16[2,256,1024]{2,1,0:T(8,128)(2,1)}, u32[]{:S(2)}) copy-start(bf16[2,256,1024]{2,1,0:T(8,128)(2,1)} %v_ref.3) | copy-start | bytes 3145732
  44.8 31.6 %copy-start.2 = (bf16[2,8192]{1,0:T(2,128)(2,1)S(1)}, bf16[2,8192]{1,0:T(2,128)(2,1)}, u32[]{:S(2)}) copy-start(bf16[2,8192]{1,0:T(2,128)(2,1)} %param.6) | copy-start | bytes 98308
  44.8 31.6 %copy-start.3 = (s32[2]{0:T(128)S(1)}, s32[2]{0:T(128)}, u32[]{:S(2)}) copy-start(s32[2]{0:T(128)} %len_ref.1) | copy-start | bytes 28
  70.8 35.4 %all-to-all-start.1 = ((bf16[32,9,16,128]{3,2,1,0:T(8,128)(2,1)}), bf16[32,9,16,128]{3,2,1,0:T(8,128)(2,1)S(1)}, u32[]{:S(2)}, u32[]{:S(2)}) async-start(bf16[32,9,16,128]{3,2,1,0:T(8,128)(2,1)} %prefix_part.1), calls=%async_computation.1 | async-start | bytes 2359296 | tf_op jit(solution)/shard_map/all_to_all | solution.py:175

commit v2 on v1

v2 whole, which is shorter than its diff:
```python
import functools

import jax
import jax.numpy as jnp
from jax import lax
from jax.experimental import pallas as pl
from jax.experimental.pallas import tpu as pltpu
from jax.sharding import PartitionSpec as P

HD = 128
LOG2E = 1.4426950408889634
NEG_FILL = -1e30
ROWS = 16
Z, X = 8, 4

NT = (((1,), (1,)), ((), ()))
NN = (((1,), (0,)), ((), ()))
TN = (((0,), (0,)), ((), ()))
VMEM = pl.BlockSpec(memory_space=pltpu.VMEM)


def dot(a, b, dims):
    return lax.dot_general(a, b, dims, preferred_element_type=jnp.float32)


def rounded(x):
    return x.astype(jnp.bfloat16).astype(jnp.float32)


def by_device(field):
    row = lax.broadcasted_iota(jnp.int32, (8, HD), 0)
    group = lax.broadcasted_iota(jnp.int32, (8, HD), 1) // ROWS
    turn = (row - group) % 8
    out = field
    for k in range(1, 8):
        moved = pltpu.roll(pltpu.roll(field, k, 0), HD - ROWS * k, 1)
        out = jnp.where(turn == k, moved, out)
    return out


def stat_rows(tops, sums):
    devices = tops.shape[0]
    high = rounded(sums)
    row = lax.broadcasted_iota(jnp.int32, (devices, ROWS, HD), 1)
    low = jnp.where(row == 2, (sums - high)[:, None], 0.0)
    rows = jnp.where(row == 0, tops[:, None], jnp.where(row == 1, high[:, None], low))
    return rows.astype(jnp.bfloat16)


def read_stats(ref):
    stats = ref[:, ref.shape[1] - 1].astype(jnp.float32)
    return stats[:, 0], stats[:, 1] + stats[:, 2]


def columns(fields):
    used = sum(f.shape[0] for f in fields)
    return jnp.concatenate(list(fields) + [jnp.zeros((HD - used, HD), jnp.float32)], axis=0).T


def suffix_head(factor, head, lens, q_ref, k_ref, v_ref, out_ref, top_ref, sum_ref):
    length = k_ref.shape[1]
    lanes = pl.ds(pl.multiple_of(head * HD, HD), HD)
    odd = lax.broadcasted_iota(jnp.int32, (ROWS, length), 0) % 2 == 1
    position = lax.broadcasted_iota(jnp.int32, (ROWS, length), 1)
    valid = position < jnp.where(odd, lens[1], lens[0])
    queries = q_ref[head]
    scores = jnp.where(odd, dot(queries, k_ref[1, :, lanes], NT), dot(queries, k_ref[0, :, lanes], NT))
    top = jnp.max(jnp.where(valid, scores, NEG_FILL), axis=1, keepdims=True)
    weights = jnp.where(valid, jnp.exp2((scores - top) * factor), 0.0).astype(jnp.bfloat16)
    total = jnp.sum(weights.astype(jnp.float32), axis=1, keepdims=True)
    outs = jnp.where(odd[:, :HD], dot(weights, v_ref[1, :, lanes], NN), dot(weights, v_ref[0, :, lanes], NN))
    out_ref[pl.ds(pl.multiple_of(head * ROWS, ROWS), ROWS)] = outs
    lane = lax.broadcasted_iota(jnp.int32, (ROWS, HD), 1)
    row = lax.broadcasted_iota(jnp.int32, (ROWS, HD), 0)
    here = lane == head * ROWS + row
    top_ref[...] = jnp.where(here, top, top_ref[...])
    sum_ref[...] = jnp.where(here, total, sum_ref[...])


def prefix_kernel(factor, parts, with_suffix, *refs):
    refs = list(refs)
    take = lambda n: [refs.pop(0) for _ in range(n)]
    if with_suffix:
        suffix_in = take(4)
    else:
        take(1)
    q_refs = take(parts)
    k_ref, v_ref = take(2)
    out_refs = take(parts)
    if with_suffix:
        suf_ref, stat_ref = take(2)
    top_ref, sum_ref = take(2)
    devices, heads = q_refs[0].shape[:2]
    span = devices * ROWS
    length = k_ref.shape[0]

    def head_part(head, pieces, shift):
        step = length // pieces
        lanes = pl.ds(pl.multiple_of(head * HD, HD), HD)
        queries = jnp.concatenate([r[:, head].reshape(span, HD) for r in q_refs], axis=0)
        scores = [dot(k_ref[i * step:(i + 1) * step, lanes], queries, NT) for i in range(pieces)]
        top = rounded(jnp.max(scores[0][:shift], axis=0, keepdims=True))
        total = None
        for i in range(pieces):
            weights = jnp.exp2((scores[i] - top) * factor).astype(jnp.bfloat16)
            values = v_ref[i * step:(i + 1) * step, lanes]
            values = jnp.concatenate([values, jnp.ones((step, ROWS), jnp.bfloat16)], axis=1)
            more = dot(values, weights, TN)
            total = more if total is None else total + more
        outs = total[:HD].T.astype(jnp.bfloat16)
        for i in range(parts):
            out_refs[i][:, head] = outs[i * span:(i + 1) * span].reshape(devices, ROWS, HD)
        top_ref[pl.ds(head, 1)] = top
        sum_ref[pl.ds(head, 1)] = total[HD:HD + 1]

    if with_suffix:
        suf_top, suf_sum = take(2)
        suf_top[...] = jnp.zeros_like(suf_top)
        suf_sum[...] = jnp.zeros_like(suf_sum)
        lens = suffix_in[0][0], suffix_in[0][1]

    @pl.loop(0, heads // 4)
    def _(i):
        for j in range(4):
            head_part(i * 4 + j, 4, 256)
            if with_suffix:
                suffix_head(factor, i * 4 + j, lens, *suffix_in[1:], suf_ref, suf_top, suf_sum)

    @pl.when(jnp.logical_not(jnp.max(sum_ref[...]) < 2.0 ** 64))
    def _():
        @pl.loop(0, heads)
        def _(i):
            head_part(i, 1, length)

    for i in range(parts):
        part = slice(i * span, (i + 1) * span)
        out_refs[i][:, heads] = stat_rows(by_device(top_ref[:, part]), by_device(sum_ref[:, part]))
    if with_suffix:
        stat_ref[0:1] = jnp.sum(suf_top[...], axis=0, keepdims=True)
        stat_ref[1:2] = jnp.sum(suf_sum[...], axis=0, keepdims=True)
        stat_ref[2:] = jnp.zeros((6, HD), jnp.float32)


def prefix_part(queries, keys, values, factor, after=None, suffix=None):
    parts = len(queries)
    devices, heads = queries[0].shape[:2]
    length = keys.shape[0]
    rows = parts * devices * ROWS
    outs = [jax.ShapeDtypeStruct((devices, heads + 1, ROWS, HD), jnp.bfloat16)] * parts
    scratch = [pltpu.VMEM((heads, rows), jnp.float32)] * 2
    if suffix is None:
        first, first_specs = [after], [pl.BlockSpec(memory_space=pl.ANY)]
    else:
        first, first_specs = list(suffix), [pl.BlockSpec(memory_space=pltpu.SMEM), VMEM, VMEM, VMEM]
        outs += [jax.ShapeDtypeStruct((heads * ROWS, HD), jnp.float32), jax.ShapeDtypeStruct((8, HD), jnp.float32)]
        scratch += [pltpu.VMEM((ROWS, HD), jnp.float32)] * 2
    return pl.pallas_call(
        functools.partial(prefix_kernel, factor, parts, suffix is not None),
        in_specs=first_specs + [VMEM] * (parts + 2),
        out_specs=[VMEM] * len(outs),
        out_shape=outs,
        scratch_shapes=scratch,
        compiler_params=pltpu.CompilerParams(vmem_limit_bytes=32 * 2**20),
        cost_estimate=pl.CostEstimate(
            flops=8 * rows * heads * length * HD,
            bytes_accessed=4 * length * heads * HD + 4 * rows * heads * HD,
            transcendentals=rows * heads * length,
        ),
        name="prefix_part",
    )(*first, *queries, keys, values)


def merge_kernel(factor, *refs):
    part_refs, out_ref = refs[:-1], refs[-1]
    devices = out_ref.shape[0]
    heads = out_ref.shape[1] - 1
    stats = [read_stats(r) for r in part_refs]
    top = functools.reduce(jnp.maximum, [s[0] for s in stats])
    scales = [jnp.exp2((s[0] - top) * factor) for s in stats]
    out_ref[:, heads] = stat_rows(top, sum(f * s[1] for f, s in zip(scales, stats)))
    turned = columns(scales)
    for dev in range(devices):
        acc = None
        for i, r in enumerate(part_refs):
            block = r[dev, :heads].reshape(heads * ROWS, HD).astype(jnp.float32)
            term = block * turned[:, i * devices + dev:i * devices + dev + 1]
            acc = term if acc is None else acc + term
        out_ref[dev, :heads] = acc.astype(jnp.bfloat16).reshape(heads, ROWS, HD)


def merge_part(parts, factor):
    return pl.pallas_call(
        functools.partial(merge_kernel, factor),
        in_specs=[VMEM] * len(parts),
        out_specs=VMEM,
        out_shape=jax.ShapeDtypeStruct(parts[0].shape, jnp.bfloat16),
        compiler_params=pltpu.CompilerParams(vmem_limit_bytes=16 * 2**20),
        name="merge_part",
    )(*parts)


def touch_kernel(after_ref, k_ref, v_ref, out_ref):
    out_ref[...] = k_ref[:ROWS, :HD] + v_ref[:ROWS, :HD]


def touch_part(after, keys, values):
    return pl.pallas_call(
        touch_kernel,
        in_specs=[pl.BlockSpec(memory_space=pl.ANY), VMEM, VMEM],
        out_specs=VMEM,
        out_shape=jax.ShapeDtypeStruct((ROWS, HD), keys.dtype),
        compiler_params=pltpu.CompilerParams(vmem_limit_bytes=16 * 2**20),
        cost_estimate=pl.CostEstimate(flops=2**30, bytes_accessed=2**23, transcendentals=0),
        name="touch_part",
    )(after, keys, values)


def combine_kernel(factor, got_ref, suf_ref, stat_ref, out_ref):
    devices = got_ref.shape[0]
    heads = got_ref.shape[1] - 1
    tops, sums = read_stats(got_ref)
    suf_top = stat_ref[0:1]
    top = jnp.maximum(jnp.max(tops, axis=0, keepdims=True), suf_top)
    scale = jnp.exp2((tops - top) * factor)
    suf_scale = jnp.exp2((suf_top - top) * factor)
    total = jnp.sum(scale * sums, axis=0, keepdims=True) + suf_scale * stat_ref[1:2]
    shares = columns([scale / total, suf_scale / total])
    acc = suf_ref[...] * shares[:, devices:devices + 1]
    for src in range(devices):
        block = got_ref[src, :heads].reshape(heads * ROWS, HD).astype(jnp.float32)
        acc += block * shares[:, src:src + 1]
    out_ref[...] = acc.astype(jnp.bfloat16)


def combine_part(got, suf_out, suf_stats, factor):
    return pl.pallas_call(
        functools.partial(combine_kernel, factor),
        in_specs=[VMEM, VMEM, VMEM],
        out_specs=VMEM,
        out_shape=jax.ShapeDtypeStruct(suf_out.shape, jnp.bfloat16),
        compiler_params=pltpu.CompilerParams(vmem_limit_bytes=16 * 2**20),
        name="combine_part",
    )(got, suf_out, suf_stats)


def shift_x(array, by):
    pairs = [(z * X + x, z * X + (x + by) % X) for z in range(Z) for x in range(X)]
    return lax.ppermute(array, "ctx", pairs)


def swap_z(array):
    groups = [[z * X + x for z in range(Z)] for x in range(X)]
    return lax.all_to_all(array, "ctx", 0, 0, axis_index_groups=groups, tiled=True)


def local(queries, prefix_keys, prefix_values, suffix_keys, suffix_values, suffix_len):
    owned, width = queries.shape
    heads = prefix_keys.shape[1] // HD
    factor = LOG2E * HD ** -0.5
    mine = queries.reshape(owned, heads, 8, HD).transpose(1, 2, 0, 3).reshape(heads, ROWS, HD)
    column = swap_z(jnp.broadcast_to(mine[None], (Z,) + mine.shape))
    before, after = shift_x(column, 1), shift_x(column, -1)
    ready = touch_part(column, prefix_keys, prefix_values)
    column, before, after = lax.optimization_barrier((column, before, after))
    across = shift_x(column, 2)
    for_before, for_after = prefix_part([before, after], prefix_keys, prefix_values, factor, after=ready)
    from_after, from_before = shift_x(for_before, -1), shift_x(for_after, 1)
    suffix = suffix_len, mine, suffix_keys, suffix_values
    for_own, for_across, suf_out, suf_stats = prefix_part(
        [column, across], prefix_keys, prefix_values, factor, suffix=suffix
    )
    from_across = shift_x(for_across, 2)
    merged = merge_part([for_own, from_after, from_before, from_across], factor)
    got = swap_z(merged)
    out = combine_part(got, suf_out, suf_stats, factor)
    return out.reshape(heads * 8, owned, HD).transpose(1, 0, 2).reshape(owned, width)


def solution(mesh):
    placed = (
        P(("grp", "ctx"), None),
        P(("grp", "ctx"), None),
        P(("grp", "ctx"), None),
        P(("grp", "ctx"), None, None),
        P(("grp", "ctx"), None, None),
        P(("grp", "ctx")),
    )
    return jax.shard_map(
        local, mesh=mesh, in_specs=placed, out_specs=P(("grp", "ctx"), None), check_vma=False
    )
```

time: 108 us -> 91.6 us (0.85)
  the two profiles are of different devices: /device:TPU:22 before, /device:TPU:26 now
where the time goes in v2:
time: 91.6 us; the launch traced here: 90.8 us
  blocking collectives  54.4 us (59%)
  Pallas kernels  14.3 us (16%)
  starting transfers between devices  11 us (12%)
  waiting for transfers between devices  5.88 us (6%)
  local copies, waits for them, and re-layouts  5.2 us (6%)
    all_to_all x2, blocking collectives, swap_z(): lax.all_to_all(array, 'ctx', 0, 0, axis_index_groups=groups, tiled=True)  54.4 us
    pallas_call x2, Pallas kernels, prefix_part(): pl.pallas_call(functools.partial(prefix_kernel, factor, parts, suffix is...  12.4 us
    ppermute x6, starting transfers between devices, shift_x(): return lax.ppermute(array, 'ctx', pairs)  11 us
    ppermute x6, waiting for transfers between devices, shift_x(): return lax.ppermute(array, 'ctx', pairs)  5.88 us
    unnamed x16, local copies, waits for them, and re-layouts  4.41 us
  transfers between devices with their start and end apart: 6, of which 2 were waited for; matrix products, arithmetic and copies ran while one was open for 0% of the time, Pallas kernels for 14%

profile of v2, /device:TPU:26, one launch (start us, length us, event | category | flops | bytes accessed | tf_op | source)
XLA Modules:
  0.0 90.8 jit_solution(9641607866094594123)
XLA Ops:
  0.0 0.8 broadcast_in_dim.2
  0.8 20.1 %all_to_all.10.refs_4_.after_ref = bf16[8,8,16,128]{3,2,1,0:T(8,128)(2,1)S(1)} all-to-all(bf16[8,8,16,128]{3,2,1,0:T(8,128)(2,1)S(1)} %broadcast_in_dim.2), channel_id=1, replica_groups={{0,4,8,12,16,20,24,28},{1,5,9,13,17,21,25,29},{2,6,10,14,18,22,26,30},{..., dimensions={0} | all-to-all | bytes 524288 | tf_op jit(solution)/shard_map/all_to_all | solution.py:253
  20.9 0.5 collective-permute-start.1
  21.5 1.5 %collective-permute-start = (bf16[8,8,16,128]{3,2,1,0:T(8,128)(2,1)S(1)}, bf16[8,8,16,128]{3,2,1,0:T(8,128)(2,1)S(1)}, u32[]{:S(2)}, u32[]{:S(2)}) collective-permute-start(bf16[8,8,16,128]{3,2,1,0:T(8,128)(2,1)S(1)} %all_to_all.10.refs_4_.after_ref), channel_id=1, source_target_pairs={{0,1},{1,2},{2,3},{3,0},{4,5},{5,6},{6,7},{7,4},{8,9},{9,10},{10,1... | collective-permute-start | bytes 786440 | tf_op jit(solution)/shard_map/ppermute | solution.py:248
  23.0 2.2 %copy-done = bf16[2048,1024]{1,0:T(8,128)(2,1)S(1)} copy-done((bf16[2048,1024]{1,0:T(8,128)(2,1)S(1)}, bf16[2048,1024]{1,0:T(8,128)(2,1)}, u32[]{:S(2)}) %copy-start) | copy-done | bytes 4194328
  25.2 2.2 %copy-done.2 = bf16[2048,1024]{1,0:T(8,128)(2,1)S(1)} copy-done((bf16[2048,1024]{1,0:T(8,128)(2,1)S(1)}, bf16[2048,1024]{1,0:T(8,128)(2,1)}, u32[]{:S(2)}) %copy-start.2) | copy-done | bytes 4194328
  27.4 0.0 copy-start.4
  27.4 0.0 copy-start.5
  27.4 0.0 copy-start.6
  27.4 0.0 copy-start.7
  27.4 0.0 collective-permute-done.1.refs_2_
  27.4 1.2 %collective-permute-done.refs_1_ = bf16[8,8,16,128]{3,2,1,0:T(8,128)(2,1)S(1)} collective-permute-done((bf16[8,8,16,128]{3,2,1,0:T(8,128)(2,1)S(1)}, bf16[8,8,16,128]{3,2,1,0:T(8,128)(2,1)S(1)}, u32[]{:S(2)}, u32[]{:S(2)}) %collective-permute-start) | collective-permute-done | bytes 262176 | tf_op jit(solution)/shard_map/ppermute | solution.py:248
  28.6 2.3 %collective-permute-start.2 = (bf16[8,8,16,128]{3,2,1,0:T(8,128)(2,1)S(1)}, bf16[8,8,16,128]{3,2,1,0:T(8,128)(2,1)S(1)}, u32[]{:S(2)}, u32[]{:S(2)}) collective-permute-start(bf16[8,8,16,128]{3,2,1,0:T(8,128)(2,1)S(1)} %all_to_all.10.refs_4_.after_ref), channel_id=1, source_target_pairs={{0,2},{1,3},{2,0},{3,1},{4,6},{5,7},{6,4},{7,5},{8,10},{9,11},{10,... | collective-permute-start | bytes 786440 | tf_op jit(solution)/shard_map/ppermute | solution.py:248
  30.8 5.5 %prefix_part.3 = (bf16[8,9,16,128]{3,2,1,0:T(8,128)(2,1)S(1)}, bf16[8,9,16,128]{3,2,1,0:T(8,128)(2,1)S(1)}) custom-call(bf16[16,128]{1,0:T(8,128)(2,1)S(1)} %touch_part.1.refs_0_, bf16[8,8,16,128]{3,2,1,0:T(8,128)(2,1)S(1)} %collective-permute-done.refs_1_, bf16[8,8,16,128]{3,2,1,0:T(8,128)(2,1)S(1)} %collective-permute-done.1.refs_2_, ...), custom_call_target="tpu_custom_call" | custom-call | flops 4294967296 | bytes 9437184 | tf_op jit(solution)/shard_map/prefix_part/pallas_call | solution.py:157
  36.3 1.3 %collective-permute-start.3 = (bf16[8,9,16,128]{3,2,1,0:T(8,128)(2,1)S(1)}, bf16[8,9,16,128]{3,2,1,0:T(8,128)(2,1)S(1)}, u32[]{:S(2)}, u32[]{:S(2)}) collective-permute-start(bf16[8,9,16,128]{3,2,1,0:T(8,128)(2,1)S(1)} %get-tuple-element.18), channel_id=1, source_target_pairs={{0,3},{1,0},{2,1},{3,2},{4,7},{5,4},{6,5},{7,6},{8,11},{9,8},{10,9... | collective-permute-start | bytes 884744 | tf_op jit(solution)/shard_map/ppermute | solution.py:248
  37.6 1.3 %collective-permute-start.4 = (bf16[8,9,16,128]{3,2,1,0:T(8,128)(2,1)S(1)}, bf16[8,9,16,128]{3,2,1,0:T(8,128)(2,1)S(1)}, u32[]{:S(2)}, u32[]{:S(2)}) collective-permute-start(bf16[8,9,16,128]{3,2,1,0:T(8,128)(2,1)S(1)} %get-tuple-element.19), channel_id=1, source_target_pairs={{0,1},{1,2},{2,3},{3,0},{4,5},{5,6},{6,7},{7,4},{8,9},{9,10},{10,1... | collective-permute-start | bytes 884744 | tf_op jit(solution)/shard_map/ppermute | solution.py:248
  39.0 6.9 %prefix_part.2 = (bf16[8,9,16,128]{3,2,1,0:T(8,128)(2,1)S(1)}, bf16[8,9,16,128]{3,2,1,0:T(8,128)(2,1)S(1)}, f32[128,128]{1,0:T(8,128)S(1)}, f32[8,128]{1,0:T(8,128)S(1)}) custom-call(s32[2]{0:T(128)S(1)} %copy-done.7, bf16[8,16,128]{2,1,0:T(8,128)(2,1)S(1)} %bitcast.11, bf16[2,256,1024]{2,1,0:T(8,128)(2,1)S(1)} %copy-done.5, ...), custom_call_target="tpu_custom_call" | custom-call | flops 4294967296 | bytes 9437184 | tf_op jit(solution)/shard_map/prefix_part/pallas_call | solution.py:157
  45.9 4.1 %collective-permute-start.5 = (bf16[8,9,16,128]{3,2,1,0:T(8,128)(2,1)S(1)}, bf16[8,9,16,128]{3,2,1,0:T(8,128)(2,1)S(1)}, u32[]{:S(2)}, u32[]{:S(2)}) collective-permute-start(bf16[8,9,16,128]{3,2,1,0:T(8,128)(2,1)S(1)} %get-tuple-element.20), channel_id=1, source_target_pairs={{0,2},{1,3},{2,0},{3,1},{4,6},{5,7},{6,4},{7,5},{8,10},{9,11},{10,... | collective-permute-start | bytes 884744 | tf_op jit(solution)/shard_map/ppermute | solution.py:248
  50.0 0.0 collective-permute-done.3.refs_1_
  50.0 0.0 collective-permute-done.4.refs_2_
  50.0 4.7 %collective-permute-done.5.refs_3_ = bf16[8,9,16,128]{3,2,1,0:T(8,128)(2,1)S(1)} collective-permute-done((bf16[8,9,16,128]{3,2,1,0:T(8,128)(2,1)S(1)}, bf16[8,9,16,128]{3,2,1,0:T(8,128)(2,1)S(1)}, u32[]{:S(2)}, u32[]{:S(2)}) %collective-permute-start.5) | collective-permute-done | bytes 294944 | tf_op jit(solution)/shard_map/ppermute | solution.py:248
  54.7 0.8 merge_part.1
  55.6 34.3 %all_to_all.11.got_ref = bf16[8,9,16,128]{3,2,1,0:T(8,128)(2,1)S(1)} all-to-all(bf16[8,9,16,128]{3,2,1,0:T(8,128)(2,1)S(1)} %merge_part.1), channel_id=1, replica_groups={{0,4,8,12,16,20,24,28},{1,5,9,13,17,21,25,29},{2,6,10,14,18,22,26,30},{..., dimensions={0} | all-to-all | bytes 589824 | tf_op jit(solution)/shard_map/all_to_all | solution.py:253
  89.8 1.0 %combine_part.1 = bf16[128,128]{1,0:T(8,128)(2,1)} custom-call(bf16[8,9,16,128]{3,2,1,0:T(8,128)(2,1)S(1)} %all_to_all.11.got_ref, f32[128,128]{1,0:T(8,128)S(1)} %get-tuple-element.21.suf_ref, f32[8,128]{1,0:T(8,128)S(1)} %get-tuple-element.22.stat_ref), custom_call_target="tpu_custom_call" | custom-call | tf_op jit(solution)/shard_map/combine_part/pallas_call | solution.py:236
  (12 shorter events, 0.0 us)
Async XLA Ops:
  20.9 6.5 %collective-permute-start.1 = (bf16[8,8,16,128]{3,2,1,0:T(8,128)(2,1)S(1)}, bf16[8,8,16,128]{3,2,1,0:T(8,128)(2,1)S(1)}, u32[]{:S(2)}, u32[]{:S(2)}) collective-permute-start(bf16[8,8,16,128]{3,2,1,0:T(8,128)(2,1)S(1)} %all_to_all.10.refs_4_.after_ref), channel_id=1, source_target_pairs={{0,3},{1,0},{2,1},{3,2},{4,7},{5,4},{6,5},{7,6},{8,11},{9,8},{10,9... | collective-permute-start | bytes 786440 | tf_op jit(solution)/shard_map/ppermute | solution.py:248
  21.5 7.1 %collective-permute-start = (bf16[8,8,16,128]{3,2,1,0:T(8,128)(2,1)S(1)}, bf16[8,8,16,128]{3,2,1,0:T(8,128)(2,1)S(1)}, u32[]{:S(2)}, u32[]{:S(2)}) collective-permute-start(bf16[8,8,16,128]{3,2,1,0:T(8,128)(2,1)S(1)} %all_to_all.10.refs_4_.after_ref), channel_id=1, source_target_pairs={{0,1},{1,2},{2,3},{3,0},{4,5},{5,6},{6,7},{7,4},{8,9},{9,10},{10,1... | collective-permute-start | bytes 786440 | tf_op jit(solution)/shard_map/ppermute | solution.py:248
  23.0 2.2 %copy-start = (bf16[2048,1024]{1,0:T(8,128)(2,1)S(1)}, bf16[2048,1024]{1,0:T(8,128)(2,1)}, u32[]{:S(2)}) copy-start(bf16[2048,1024]{1,0:T(8,128)(2,1)} %refs_3_.3) | copy-start | bytes 12582916
  25.2 2.2 %copy-start.2 = (bf16[2048,1024]{1,0:T(8,128)(2,1)S(1)}, bf16[2048,1024]{1,0:T(8,128)(2,1)}, u32[]{:S(2)}) copy-start(bf16[2048,1024]{1,0:T(8,128)(2,1)} %refs_4_.1) | copy-start | bytes 12582916
  27.3 3.5 %copy-start.1 = (bf16[2048,1024]{1,0:T(8,128)(2,1)S(1)}, bf16[2048,1024]{1,0:T(8,128)(2,1)}, u32[]{:S(2)}) copy-start(bf16[2048,1024]{1,0:T(8,128)(2,1)} %refs_3_.3) | copy-start | bytes 12582916
  27.3 3.5 %copy-start.3 = (bf16[2048,1024]{1,0:T(8,128)(2,1)S(1)}, bf16[2048,1024]{1,0:T(8,128)(2,1)}, u32[]{:S(2)}) copy-start(bf16[2048,1024]{1,0:T(8,128)(2,1)} %refs_4_.1) | copy-start | bytes 12582916
  27.4 11.6 %copy-start.4 = (bf16[2,8192]{1,0:T(2,128)(2,1)S(1)}, bf16[2,8192]{1,0:T(2,128)(2,1)}, u32[]{:S(2)}) copy-start(bf16[2,8192]{1,0:T(2,128)(2,1)} %param.6) | copy-start | bytes 98308
  27.4 11.6 %copy-start.5 = (bf16[2,256,1024]{2,1,0:T(8,128)(2,1)S(1)}, bf16[2,256,1024]{2,1,0:T(8,128)(2,1)}, u32[]{:S(2)}) copy-start(bf16[2,256,1024]{2,1,0:T(8,128)(2,1)} %refs_2_.1) | copy-start | bytes 3145732
  27.4 11.6 %copy-start.6 = (bf16[2,256,1024]{2,1,0:T(8,128)(2,1)S(1)}, bf16[2,256,1024]{2,1,0:T(8,128)(2,1)}, u32[]{:S(2)}) copy-start(bf16[2,256,1024]{2,1,0:T(8,128)(2,1)} %refs_3_.2) | copy-start | bytes 3145732
  27.4 11.6 %copy-start.7 = (s32[2]{0:T(128)S(1)}, s32[2]{0:T(128)}, u32[]{:S(2)}) copy-start(s32[2]{0:T(128)} %refs_0_.1) | copy-start | bytes 28
  28.6 10.4 %collective-permute-start.2 = (bf16[8,8,16,128]{3,2,1,0:T(8,128)(2,1)S(1)}, bf16[8,8,16,128]{3,2,1,0:T(8,128)(2,1)S(1)}, u32[]{:S(2)}, u32[]{:S(2)}) collective-permute-start(bf16[8,8,16,128]{3,2,1,0:T(8,128)(2,1)S(1)} %all_to_all.10.refs_4_.after_ref), channel_id=1, source_target_pairs={{0,2},{1,3},{2,0},{3,1},{4,6},{5,7},{6,4},{7,5},{8,10},{9,11},{10,... | collective-permute-start | bytes 786440 | tf_op jit(solution)/shard_map/ppermute | solution.py:248
  36.3 13.7 %collective-permute-start.3 = (bf16[8,9,16,128]{3,2,1,0:T(8,128)(2,1)S(1)}, bf16[8,9,16,128]{3,2,1,0:T(8,128)(2,1)S(1)}, u32[]{:S(2)}, u32[]{:S(2)}) collective-permute-start(bf16[8,9,16,128]{3,2,1,0:T(8,128)(2,1)S(1)} %get-tuple-element.18), channel_id=1, source_target_pairs={{0,3},{1,0},{2,1},{3,2},{4,7},{5,4},{6,5},{7,6},{8,11},{9,8},{10,9... | collective-permute-start | bytes 884744 | tf_op jit(solution)/shard_map/ppermute | solution.py:248
  37.6 12.4 %collective-permute-start.4 = (bf16[8,9,16,128]{3,2,1,0:T(8,128)(2,1)S(1)}, bf16[8,9,16,128]{3,2,1,0:T(8,128)(2,1)S(1)}, u32[]{:S(2)}, u32[]{:S(2)}) collective-permute-start(bf16[8,9,16,128]{3,2,1,0:T(8,128)(2,1)S(1)} %get-tuple-element.19), channel_id=1, source_target_pairs={{0,1},{1,2},{2,3},{3,0},{4,5},{5,6},{6,7},{7,4},{8,9},{9,10},{10,1... | collective-permute-start | bytes 884744 | tf_op jit(solution)/shard_map/ppermute | solution.py:248
  45.9 8.8 %collective-permute-start.5 = (bf16[8,9,16,128]{3,2,1,0:T(8,128)(2,1)S(1)}, bf16[8,9,16,128]{3,2,1,0:T(8,128)(2,1)S(1)}, u32[]{:S(2)}, u32[]{:S(2)}) collective-permute-start(bf16[8,9,16,128]{3,2,1,0:T(8,128)(2,1)S(1)} %get-tuple-element.20), channel_id=1, source_target_pairs={{0,2},{1,3},{2,0},{3,1},{4,6},{5,7},{6,4},{7,5},{8,10},{9,11},{10,... | collective-permute-start | bytes 884744 | tf_op jit(solution)/shard_map/ppermute | solution.py:248

commit v3 on v2

--- a/solution.py
+++ b/solution.py
@@ -57,39 +57,11 @@
     return jnp.concatenate(list(fields) + [jnp.zeros((HD - used, HD), jnp.float32)], axis=0).T
 
 
-def suffix_head(factor, head, lens, q_ref, k_ref, v_ref, out_ref, top_ref, sum_ref):
-    length = k_ref.shape[1]
-    lanes = pl.ds(pl.multiple_of(head * HD, HD), HD)
-    odd = lax.broadcasted_iota(jnp.int32, (ROWS, length), 0) % 2 == 1
-    position = lax.broadcasted_iota(jnp.int32, (ROWS, length), 1)
-    valid = position < jnp.where(odd, lens[1], lens[0])
-    queries = q_ref[head]
-    scores = jnp.where(odd, dot(queries, k_ref[1, :, lanes], NT), dot(queries, k_ref[0, :, lanes], NT))
-    top = jnp.max(jnp.where(valid, scores, NEG_FILL), axis=1, keepdims=True)
-    weights = jnp.where(valid, jnp.exp2((scores - top) * factor), 0.0).astype(jnp.bfloat16)
-    total = jnp.sum(weights.astype(jnp.float32), axis=1, keepdims=True)
-    outs = jnp.where(odd[:, :HD], dot(weights, v_ref[1, :, lanes], NN), dot(weights, v_ref[0, :, lanes], NN))
-    out_ref[pl.ds(pl.multiple_of(head * ROWS, ROWS), ROWS)] = outs
-    lane = lax.broadcasted_iota(jnp.int32, (ROWS, HD), 1)
-    row = lax.broadcasted_iota(jnp.int32, (ROWS, HD), 0)
-    here = lane == head * ROWS + row
-    top_ref[...] = jnp.where(here, top, top_ref[...])
-    sum_ref[...] = jnp.where(here, total, sum_ref[...])
-
-
-def prefix_kernel(factor, parts, with_suffix, *refs):
-    refs = list(refs)
-    take = lambda n: [refs.pop(0) for _ in range(n)]
-    if with_suffix:
-        suffix_in = take(4)
-    else:
-        take(1)
-    q_refs = take(parts)
-    k_ref, v_ref = take(2)
-    out_refs = take(parts)
-    if with_suffix:
-        suf_ref, stat_ref = take(2)
-    top_ref, sum_ref = take(2)
+def prefix_kernel(factor, parts, after_ref, *refs):
+    q_refs = refs[:parts]
+    k_ref, v_ref = refs[parts:parts + 2]
+    out_refs = refs[parts + 2:2 * parts + 2]
+    top_ref, sum_ref = refs[2 * parts + 2:]
     devices, heads = q_refs[0].shape[:2]
     span = devices * ROWS
     length = k_ref.shape[0]
@@ -113,18 +85,10 @@
         top_ref[pl.ds(head, 1)] = top
         sum_ref[pl.ds(head, 1)] = total[HD:HD + 1]
 
-    if with_suffix:
-        suf_top, suf_sum = take(2)
-        suf_top[...] = jnp.zeros_like(suf_top)
-        suf_sum[...] = jnp.zeros_like(suf_sum)
-        lens = suffix_in[0][0], suffix_in[0][1]
-
     @pl.loop(0, heads // 4)
     def _(i):
         for j in range(4):
             head_part(i * 4 + j, 4, 256)
-            if with_suffix:
-                suffix_head(factor, i * 4 + j, lens, *suffix_in[1:], suf_ref, suf_top, suf_sum)
 
     @pl.when(jnp.logical_not(jnp.max(sum_ref[...]) < 2.0 ** 64))
     def _():
@@ -135,31 +99,19 @@
     for i in range(parts):
         part = slice(i * span, (i + 1) * span)
         out_refs[i][:, heads] = stat_rows(by_device(top_ref[:, part]), by_device(sum_ref[:, part]))
-    if with_suffix:
-        stat_ref[0:1] = jnp.sum(suf_top[...], axis=0, keepdims=True)
-        stat_ref[1:2] = jnp.sum(suf_sum[...], axis=0, keepdims=True)
-        stat_ref[2:] = jnp.zeros((6, HD), jnp.float32)
-
-
-def prefix_part(queries, keys, values, factor, after=None, suffix=None):
+
+
+def prefix_part(after, queries, keys, values, factor):
     parts = len(queries)
     devices, heads = queries[0].shape[:2]
     length = keys.shape[0]
     rows = parts * devices * ROWS
-    outs = [jax.ShapeDtypeStruct((devices, heads + 1, ROWS, HD), jnp.bfloat16)] * parts
-    scratch = [pltpu.VMEM((heads, rows), jnp.float32)] * 2
-    if suffix is None:
-        first, first_specs = [after], [pl.BlockSpec(memory_space=pl.ANY)]
-    else:
-        first, first_specs = list(suffix), [pl.BlockSpec(memory_space=pltpu.SMEM), VMEM, VMEM, VMEM]
-        outs += [jax.ShapeDtypeStruct((heads * ROWS, HD), jnp.float32), jax.ShapeDtypeStruct((8, HD), jnp.float32)]
-        scratch += [pltpu.VMEM((ROWS, HD), jnp.float32)] * 2
-    return pl.pallas_call(
-        functools.partial(prefix_kernel, factor, parts, suffix is not None),
-        in_specs=first_specs + [VMEM] * (parts + 2),
-        out_specs=[VMEM] * len(outs),
-        out_shape=outs,
-        scratch_shapes=scratch,
+    return pl.pallas_call(
+        functools.partial(prefix_kernel, factor, parts),
+        in_specs=[pl.BlockSpec(memory_space=pl.ANY)] + [VMEM] * (parts + 2),
+        out_specs=[VMEM] * parts,
+        out_shape=[jax.ShapeDtypeStruct((devices, heads + 1, ROWS, HD), jnp.bfloat16)] * parts,
+        scratch_shapes=[pltpu.VMEM((heads, rows), jnp.float32)] * 2,
         compiler_params=pltpu.CompilerParams(vmem_limit_bytes=32 * 2**20),
         cost_estimate=pl.CostEstimate(
             flops=8 * rows * heads * length * HD,
@@ -167,7 +119,67 @@
             transcendentals=rows * heads * length,
         ),
         name="prefix_part",
-    )(*first, *queries, keys, values)
+    )(after, *queries, keys, values)
+
+
+def spread_kernel(q_ref, out_ref):
+    for i in range(out_ref.shape[0]):
+        out_ref[i] = q_ref[...]
+
+
+def spread_part(queries, copies):
+    return pl.pallas_call(
+        spread_kernel,
+        in_specs=[VMEM],
+        out_specs=VMEM,
+        out_shape=jax.ShapeDtypeStruct((copies,) + queries.shape, queries.dtype),
+        compiler_params=pltpu.CompilerParams(vmem_limit_bytes=8 * 2**20),
+        cost_estimate=pl.CostEstimate(flops=20 * 2**30, bytes_accessed=2**25, transcendentals=0),
+        name="spread_part",
+    )(queries)
+
+
+def suffix_kernel(factor, len_ref, after_ref, q_ref, sk_ref, sv_ref, k_ref, v_ref, out_ref, stat_ref):
+    heads = q_ref.shape[0]
+    length = sk_ref.shape[1]
+    odd = lax.broadcasted_iota(jnp.int32, (ROWS, length), 0) % 2 == 1
+    position = lax.broadcasted_iota(jnp.int32, (ROWS, length), 1)
+    valid = position < jnp.where(odd, len_ref[1], len_ref[0])
+    lane = lax.broadcasted_iota(jnp.int32, (ROWS, HD), 1)
+    row = lax.broadcasted_iota(jnp.int32, (ROWS, HD), 0)
+    maxima = jnp.zeros((ROWS, HD), jnp.float32)
+    sums = jnp.zeros((ROWS, HD), jnp.float32)
+    for head in range(heads):
+        cols = slice(head * HD, (head + 1) * HD)
+        queries = q_ref[head]
+        scores = jnp.where(odd, dot(queries, sk_ref[1, :, cols], NT), dot(queries, sk_ref[0, :, cols], NT))
+        top = jnp.max(jnp.where(valid, scores, NEG_FILL), axis=1, keepdims=True)
+        weights = jnp.where(valid, jnp.exp2((scores - top) * factor), 0.0).astype(jnp.bfloat16)
+        total = jnp.sum(weights.astype(jnp.float32), axis=1, keepdims=True)
+        outs = jnp.where(odd[:, :HD], dot(weights, sv_ref[1, :, cols], NN), dot(weights, sv_ref[0, :, cols], NN))
+        out_ref[head * ROWS:(head + 1) * ROWS] = outs
+        here = lane == head * ROWS + row
+        maxima += jnp.where(here, top, 0.0)
+        sums += jnp.where(here, total, 0.0)
+    stat_ref[0:1] = jnp.sum(maxima, axis=0, keepdims=True)
+    stat_ref[1:2] = jnp.sum(sums, axis=0, keepdims=True)
+    stat_ref[2:] = jnp.zeros((6, HD), jnp.float32)
+
+
+def suffix_part(lengths, after, queries, suffix_keys, suffix_values, keys, values, factor):
+    heads = queries.shape[0]
+    return pl.pallas_call(
+        functools.partial(suffix_kernel, factor),
+        in_specs=[pl.BlockSpec(memory_space=pltpu.SMEM), pl.BlockSpec(memory_space=pl.ANY)] + [VMEM] * 5,
+        out_specs=[VMEM] * 2,
+        out_shape=[
+            jax.ShapeDtypeStruct((heads * ROWS, HD), jnp.float32),
+            jax.ShapeDtypeStruct((8, HD), jnp.float32),
+        ],
+        compiler_params=pltpu.CompilerParams(vmem_limit_bytes=16 * 2**20),
+        cost_estimate=pl.CostEstimate(flops=2**30, bytes_accessed=2**23, transcendentals=2**16),
+        name="suffix_part",
+    )(lengths, after, queries, suffix_keys, suffix_values, keys, values)
 
 
 def merge_kernel(factor, *refs):
@@ -199,22 +211,6 @@
     )(*parts)
 
 
-def touch_kernel(after_ref, k_ref, v_ref, out_ref):
-    out_ref[...] = k_ref[:ROWS, :HD] + v_ref[:ROWS, :HD]
-
-
-def touch_part(after, keys, values):
-    return pl.pallas_call(
-        touch_kernel,
-        in_specs=[pl.BlockSpec(memory_space=pl.ANY), VMEM, VMEM],
-        out_specs=VMEM,
-        out_shape=jax.ShapeDtypeStruct((ROWS, HD), keys.dtype),
-        compiler_params=pltpu.CompilerParams(vmem_limit_bytes=16 * 2**20),
-        cost_estimate=pl.CostEstimate(flops=2**30, bytes_accessed=2**23, transcendentals=0),
-        name="touch_part",
-    )(after, keys, values)
-
-
 def combine_kernel(factor, got_ref, suf_ref, stat_ref, out_ref):
     devices = got_ref.shape[0]
     heads = got_ref.shape[1] - 1
@@ -258,17 +254,16 @@
     heads = prefix_keys.shape[1] // HD
     factor = LOG2E * HD ** -0.5
     mine = queries.reshape(owned, heads, 8, HD).transpose(1, 2, 0, 3).reshape(heads, ROWS, HD)
-    column = swap_z(jnp.broadcast_to(mine[None], (Z,) + mine.shape))
+    column = swap_z(spread_part(mine, Z))
     before, after = shift_x(column, 1), shift_x(column, -1)
-    ready = touch_part(column, prefix_keys, prefix_values)
+    suf_out, suf_stats = suffix_part(
+        suffix_len, column, mine, suffix_keys, suffix_values, prefix_keys, prefix_values, factor
+    )
     column, before, after = lax.optimization_barrier((column, before, after))
     across = shift_x(column, 2)
-    for_before, for_after = prefix_part([before, after], prefix_keys, prefix_values, factor, after=ready)
+    for_before, for_after = prefix_part(suf_stats, [before, after], prefix_keys, prefix_values, factor)
     from_after, from_before = shift_x(for_before, -1), shift_x(for_after, 1)
-    suffix = suffix_len, mine, suffix_keys, suffix_values
-    for_own, for_across, suf_out, suf_stats = prefix_part(
-        [column, across], prefix_keys, prefix_values, factor, suffix=suffix
-    )
+    for_own, for_across = prefix_part(suf_stats, [column, across], prefix_keys, prefix_values, factor)
     from_across = shift_x(for_across, 2)
     merged = merge_part([for_own, from_after, from_before, from_across], factor)
     got = swap_z(merged)

time: 91.6 us -> 90.7 us (level)
  the two profiles are of different devices: /device:TPU:26 before, /device:TPU:22 now
where the time goes in v3:
time: 90.7 us; the launch traced here: 89.8 us
  blocking collectives  55.5 us (61%)
  Pallas kernels  15.3 us (17%)
  starting transfers between devices  9.66 us (11%)
  waiting for transfers between devices  8.43 us (9%)
    all_to_all x2, blocking collectives, swap_z(): lax.all_to_all(array, 'ctx', 0, 0, axis_index_groups=groups, tiled=True)  55.5 us
    pallas_call x2, Pallas kernels, prefix_part(): pl.pallas_call(functools.partial(prefix_kernel, factor, parts), in_specs=...  10.9 us
    ppermute x6, starting transfers between devices, shift_x(): return lax.ppermute(array, 'ctx', pairs)  9.66 us
    ppermute x6, waiting for transfers between devices, shift_x(): return lax.ppermute(array, 'ctx', pairs)  8.43 us
    pallas_call x1, Pallas kernels, suffix_part(): pl.pallas_call(functools.partial(suffix_kernel, factor), in_specs=[pl.Blo...  2.54 us
  transfers between devices with their start and end apart: 6, of which 3 were waited for; matrix products, arithmetic and copies ran while one was open for 0% of the time, Pallas kernels for 15%

profile of v3, /device:TPU:22, one launch (start us, length us, event | category | flops | bytes accessed | tf_op | source)
XLA Modules:
  0.0 89.8 jit_solution(16272869158235319303)
XLA Ops:
  0.0 0.8 copy-done.4
  0.8 0.0 copy-start.5
  0.8 0.0 copy-start.6
  0.8 20.4 %all_to_all.10.after_ref.refs_0_ = bf16[8,8,16,128]{3,2,1,0:T(8,128)(2,1)S(1)} all-to-all(bf16[8,8,16,128]{3,2,1,0:T(8,128)(2,1)S(1)} %spread_part.1), channel_id=1, replica_groups={{0,4,8,12,16,20,24,28},{1,5,9,13,17,21,25,29},{2,6,10,14,18,22,26,30},{..., dimensions={0} | all-to-all | bytes 524288 | tf_op jit(solution)/shard_map/all_to_all | solution.py:249
  21.2 0.8 collective-permute-start.1
  22.1 2.4 %collective-permute-start = (bf16[8,8,16,128]{3,2,1,0:T(8,128)(2,1)S(1)}, bf16[8,8,16,128]{3,2,1,0:T(8,128)(2,1)S(1)}, u32[]{:S(2)}, u32[]{:S(2)}) collective-permute-start(bf16[8,8,16,128]{3,2,1,0:T(8,128)(2,1)S(1)} %all_to_all.10.after_ref.refs_0_), channel_id=1, source_target_pairs={{0,1},{1,2},{2,3},{3,0},{4,5},{5,6},{6,7},{7,4},{8,9},{9,10},{10,1... | collective-permute-start | bytes 786440 | tf_op jit(solution)/shard_map/ppermute | solution.py:244
  24.5 0.0 copy-done
  24.5 0.0 copy-done.2
  24.5 2.5 %suffix_part.1 = (f32[128,128]{1,0:T(8,128)S(1)}, f32[8,128]{1,0:T(8,128)S(1)}) custom-call(s32[2]{0:T(128)S(1)} %copy-done.6, bf16[8,8,16,128]{3,2,1,0:T(8,128)(2,1)S(1)} %all_to_all.10.after_ref.refs_0_, bf16[8,16,128]{2,1,0:T(8,128)(2,1)S(1)} %bitcast.11, bf16[2,256,1024]{2,1,0:T(8,128)(2,1)S(1)} %copy-done.2, bf16[2,256,1024]{2,1,0:T(8,128)(2,1)S(1)} %copy-done.3, ...), custom_call_target="tpu_custom_call" | custom-call | flops 1073741824 | bytes 8388608 | tf_op jit(solution)/shard_map/suffix_part/pallas_call | solution.py:171
  27.1 1.8 %collective-permute-done.1.refs_1_ = bf16[8,8,16,128]{3,2,1,0:T(8,128)(2,1)S(1)} collective-permute-done((bf16[8,8,16,128]{3,2,1,0:T(8,128)(2,1)S(1)}, bf16[8,8,16,128]{3,2,1,0:T(8,128)(2,1)S(1)}, u32[]{:S(2)}, u32[]{:S(2)}) %collective-permute-start.1) | collective-permute-done | bytes 262176 | tf_op jit(solution)/shard_map/ppermute | solution.py:244
  28.8 0.0 collective-permute-done.refs_0_
  28.8 1.5 %collective-permute-start.2 = (bf16[8,8,16,128]{3,2,1,0:T(8,128)(2,1)S(1)}, bf16[8,8,16,128]{3,2,1,0:T(8,128)(2,1)S(1)}, u32[]{:S(2)}, u32[]{:S(2)}) collective-permute-start(bf16[8,8,16,128]{3,2,1,0:T(8,128)(2,1)S(1)} %all_to_all.10.after_ref.refs_0_), channel_id=1, source_target_pairs={{0,2},{1,3},{2,0},{3,1},{4,6},{5,7},{6,4},{7,5},{8,10},{9,11},{10,... | collective-permute-start | bytes 786440 | tf_op jit(solution)/shard_map/ppermute | solution.py:244
  30.3 5.5 %prefix_part.3 = (bf16[8,9,16,128]{3,2,1,0:T(8,128)(2,1)S(1)}, bf16[8,9,16,128]{3,2,1,0:T(8,128)(2,1)S(1)}) custom-call(f32[8,128]{1,0:T(8,128)S(1)} %get-tuple-element.14.after_ref.stat_ref, bf16[8,8,16,128]{3,2,1,0:T(8,128)(2,1)S(1)} %collective-permute-done.refs_0_, bf16[8,8,16,128]{3,2,1,0:T(8,128)(2,1)S(1)} %collective-permute-done.1.refs_1_, ...), custom_call_target="tpu_custom_call" | custom-call | flops 4294967296 | bytes 9437184 | tf_op jit(solution)/shard_map/prefix_part/pallas_call | solution.py:109
  35.8 2.7 %collective-permute-start.3 = (bf16[8,9,16,128]{3,2,1,0:T(8,128)(2,1)S(1)}, bf16[8,9,16,128]{3,2,1,0:T(8,128)(2,1)S(1)}, u32[]{:S(2)}, u32[]{:S(2)}) collective-permute-start(bf16[8,9,16,128]{3,2,1,0:T(8,128)(2,1)S(1)} %get-tuple-element.19), channel_id=1, source_target_pairs={{0,3},{1,0},{2,1},{3,2},{4,7},{5,4},{6,5},{7,6},{8,11},{9,8},{10,9... | collective-permute-start | bytes 884744 | tf_op jit(solution)/shard_map/ppermute | solution.py:244
  38.5 0.6 collective-permute-start.4
  39.1 0.0 collective-permute-done.2.refs_1_
  39.1 5.5 %prefix_part.2 = (bf16[8,9,16,128]{3,2,1,0:T(8,128)(2,1)S(1)}, bf16[8,9,16,128]{3,2,1,0:T(8,128)(2,1)S(1)}) custom-call(f32[8,128]{1,0:T(8,128)S(1)} %get-tuple-element.14.after_ref.stat_ref, bf16[8,8,16,128]{3,2,1,0:T(8,128)(2,1)S(1)} %all_to_all.10.after_ref.refs_0_, bf16[8,8,16,128]{3,2,1,0:T(8,128)(2,1)S(1)} %collective-permute-done.2.refs_1_, ...), custom_call_target="tpu_custom_call" | custom-call | flops 4294967296 | bytes 9437184 | tf_op jit(solution)/shard_map/prefix_part/pallas_call | solution.py:109
  44.6 1.7 %collective-permute-start.5 = (bf16[8,9,16,128]{3,2,1,0:T(8,128)(2,1)S(1)}, bf16[8,9,16,128]{3,2,1,0:T(8,128)(2,1)S(1)}, u32[]{:S(2)}, u32[]{:S(2)}) collective-permute-start(bf16[8,9,16,128]{3,2,1,0:T(8,128)(2,1)S(1)} %get-tuple-element.21), channel_id=1, source_target_pairs={{0,2},{1,3},{2,0},{3,1},{4,6},{5,7},{6,4},{7,5},{8,10},{9,11},{10,... | collective-permute-start | bytes 884744 | tf_op jit(solution)/shard_map/ppermute | solution.py:244
  46.2 0.0 collective-permute-done.3.refs_1_
  46.2 1.5 %collective-permute-done.4.refs_2_ = bf16[8,9,16,128]{3,2,1,0:T(8,128)(2,1)S(1)} collective-permute-done((bf16[8,9,16,128]{3,2,1,0:T(8,128)(2,1)S(1)}, bf16[8,9,16,128]{3,2,1,0:T(8,128)(2,1)S(1)}, u32[]{:S(2)}, u32[]{:S(2)}) %collective-permute-start.4) | collective-permute-done | bytes 294944 | tf_op jit(solution)/shard_map/ppermute | solution.py:244
  47.7 5.1 %collective-permute-done.5.refs_3_ = bf16[8,9,16,128]{3,2,1,0:T(8,128)(2,1)S(1)} collective-permute-done((bf16[8,9,16,128]{3,2,1,0:T(8,128)(2,1)S(1)}, bf16[8,9,16,128]{3,2,1,0:T(8,128)(2,1)S(1)}, u32[]{:S(2)}, u32[]{:S(2)}) %collective-permute-start.5) | collective-permute-done | bytes 294944 | tf_op jit(solution)/shard_map/ppermute | solution.py:244
  52.9 0.8 merge_part.1
  53.7 35.1 %all_to_all.11.got_ref = bf16[8,9,16,128]{3,2,1,0:T(8,128)(2,1)S(1)} all-to-all(bf16[8,9,16,128]{3,2,1,0:T(8,128)(2,1)S(1)} %merge_part.1), channel_id=1, replica_groups={{0,4,8,12,16,20,24,28},{1,5,9,13,17,21,25,29},{2,6,10,14,18,22,26,30},{..., dimensions={0} | all-to-all | bytes 589824 | tf_op jit(solution)/shard_map/all_to_all | solution.py:249
  88.8 1.0 %combine_part.1 = bf16[128,128]{1,0:T(8,128)(2,1)} custom-call(bf16[8,9,16,128]{3,2,1,0:T(8,128)(2,1)S(1)} %all_to_all.11.got_ref, f32[128,128]{1,0:T(8,128)S(1)} %get-tuple-element.22.suf_ref, f32[8,128]{1,0:T(8,128)S(1)} %get-tuple-element.14.after_ref.stat_ref), custom_call_target="tpu_custom_call" | custom-call | tf_op jit(solution)/shard_map/combine_part/pallas_call | solution.py:232
  (10 shorter events, 0.1 us)
Async XLA Ops:
  0.0 0.8 copy-start.4
  0.8 23.7 %copy-start = (bf16[2048,1024]{1,0:T(8,128)(2,1)S(1)}, bf16[2048,1024]{1,0:T(8,128)(2,1)}, u32[]{:S(2)}) copy-start(bf16[2048,1024]{1,0:T(8,128)(2,1)} %refs_2_.3) | copy-start | bytes 12582916
  0.8 23.7 %copy-start.1 = (bf16[2048,1024]{1,0:T(8,128)(2,1)S(1)}, bf16[2048,1024]{1,0:T(8,128)(2,1)}, u32[]{:S(2)}) copy-start(bf16[2048,1024]{1,0:T(8,128)(2,1)} %refs_3_.3) | copy-start | bytes 12582916
  0.8 23.7 %copy-start.2 = (bf16[2,256,1024]{2,1,0:T(8,128)(2,1)S(1)}, bf16[2,256,1024]{2,1,0:T(8,128)(2,1)}, u32[]{:S(2)}) copy-start(bf16[2,256,1024]{2,1,0:T(8,128)(2,1)} %sk_ref.1) | copy-start | bytes 3145732
  0.8 23.7 %copy-start.3 = (bf16[2,256,1024]{2,1,0:T(8,128)(2,1)S(1)}, bf16[2,256,1024]{2,1,0:T(8,128)(2,1)}, u32[]{:S(2)}) copy-start(bf16[2,256,1024]{2,1,0:T(8,128)(2,1)} %sv_ref.1) | copy-start | bytes 3145732
  0.8 23.7 %copy-start.5 = (bf16[2,8192]{1,0:T(2,128)(2,1)S(1)}, bf16[2,8192]{1,0:T(2,128)(2,1)}, u32[]{:S(2)}) copy-start(bf16[2,8192]{1,0:T(2,128)(2,1)} %param.6) | copy-start | bytes 98308
  0.8 23.7 %copy-start.6 = (s32[2]{0:T(128)S(1)}, s32[2]{0:T(128)}, u32[]{:S(2)}) copy-start(s32[2]{0:T(128)} %len_ref.1) | copy-start | bytes 28
  21.2 7.6 %collective-permute-start.1 = (bf16[8,8,16,128]{3,2,1,0:T(8,128)(2,1)S(1)}, bf16[8,8,16,128]{3,2,1,0:T(8,128)(2,1)S(1)}, u32[]{:S(2)}, u32[]{:S(2)}) collective-permute-start(bf16[8,8,16,128]{3,2,1,0:T(8,128)(2,1)S(1)} %all_to_all.10.after_ref.refs_0_), channel_id=1, source_target_pairs={{0,3},{1,0},{2,1},{3,2},{4,7},{5,4},{6,5},{7,6},{8,11},{9,8},{10,9... | collective-permute-start | bytes 786440 | tf_op jit(solution)/shard_map/ppermute | solution.py:244
  22.1 6.8 %collective-permute-start = (bf16[8,8,16,128]{3,2,1,0:T(8,128)(2,1)S(1)}, bf16[8,8,16,128]{3,2,1,0:T(8,128)(2,1)S(1)}, u32[]{:S(2)}, u32[]{:S(2)}) collective-permute-start(bf16[8,8,16,128]{3,2,1,0:T(8,128)(2,1)S(1)} %all_to_all.10.after_ref.refs_0_), channel_id=1, source_target_pairs={{0,1},{1,2},{2,3},{3,0},{4,5},{5,6},{6,7},{7,4},{8,9},{9,10},{10,1... | collective-permute-start | bytes 786440 | tf_op jit(solution)/shard_map/ppermute | solution.py:244
  28.8 10.3 %collective-permute-start.2 = (bf16[8,8,16,128]{3,2,1,0:T(8,128)(2,1)S(1)}, bf16[8,8,16,128]{3,2,1,0:T(8,128)(2,1)S(1)}, u32[]{:S(2)}, u32[]{:S(2)}) collective-permute-start(bf16[8,8,16,128]{3,2,1,0:T(8,128)(2,1)S(1)} %all_to_all.10.after_ref.refs_0_), channel_id=1, source_target_pairs={{0,2},{1,3},{2,0},{3,1},{4,6},{5,7},{6,4},{7,5},{8,10},{9,11},{10,... | collective-permute-start | bytes 786440 | tf_op jit(solution)/shard_map/ppermute | solution.py:244
  35.8 10.4 %collective-permute-start.3 = (bf16[8,9,16,128]{3,2,1,0:T(8,128)(2,1)S(1)}, bf16[8,9,16,128]{3,2,1,0:T(8,128)(2,1)S(1)}, u32[]{:S(2)}, u32[]{:S(2)}) collective-permute-start(bf16[8,9,16,128]{3,2,1,0:T(8,128)(2,1)S(1)} %get-tuple-element.19), channel_id=1, source_target_pairs={{0,3},{1,0},{2,1},{3,2},{4,7},{5,4},{6,5},{7,6},{8,11},{9,8},{10,9... | collective-permute-start | bytes 884744 | tf_op jit(solution)/shard_map/ppermute | solution.py:244
  38.5 9.3 %collective-permute-start.4 = (bf16[8,9,16,128]{3,2,1,0:T(8,128)(2,1)S(1)}, bf16[8,9,16,128]{3,2,1,0:T(8,128)(2,1)S(1)}, u32[]{:S(2)}, u32[]{:S(2)}) collective-permute-start(bf16[8,9,16,128]{3,2,1,0:T(8,128)(2,1)S(1)} %get-tuple-element.20), channel_id=1, source_target_pairs={{0,1},{1,2},{2,3},{3,0},{4,5},{5,6},{6,7},{7,4},{8,9},{9,10},{10,1... | collective-permute-start | bytes 884744 | tf_op jit(solution)/shard_map/ppermute | solution.py:244
  44.6 8.3 %collective-permute-start.5 = (bf16[8,9,16,128]{3,2,1,0:T(8,128)(2,1)S(1)}, bf16[8,9,16,128]{3,2,1,0:T(8,128)(2,1)S(1)}, u32[]{:S(2)}, u32[]{:S(2)}) collective-permute-start(bf16[8,9,16,128]{3,2,1,0:T(8,128)(2,1)S(1)} %get-tuple-element.21), channel_id=1, source_target_pairs={{0,2},{1,3},{2,0},{3,1},{4,6},{5,7},{6,4},{7,5},{8,10},{9,11},{10,... | collective-permute-start | bytes 884744 | tf_op jit(solution)/shard_map/ppermute | solution.py:244

commit v4 on v3

--- a/solution.py
+++ b/solution.py
@@ -52,6 +52,19 @@
     return stats[:, 0], stats[:, 1] + stats[:, 2]
 
 
+def write_packed_stats(ref, tops, sums):
+    last = ref.shape[0] - 2
+    high = rounded(sums)
+    ref[last] = jnp.concatenate([tops, high], axis=0).astype(jnp.bfloat16)
+    ref[last + 1] = jnp.concatenate([sums - high, jnp.zeros_like(sums)], axis=0).astype(jnp.bfloat16)
+
+
+def read_packed_stats(ref):
+    last = ref.shape[0] - 2
+    first, second = ref[last].astype(jnp.float32), ref[last + 1].astype(jnp.float32)
+    return first[:8], first[8:] + second[:8]
+
+
 def columns(fields):
     used = sum(f.shape[0] for f in fields)
     return jnp.concatenate(list(fields) + [jnp.zeros((HD - used, HD), jnp.float32)], axis=0).T
@@ -66,9 +79,34 @@
     span = devices * ROWS
     length = k_ref.shape[0]
 
+    def pair_part(pair, pieces, shift):
+        step = length // pieces
+        lanes = slice(pair * 2 * HD, (pair + 1) * 2 * HD)
+        both = [q_refs[0][:, pair * 2 + j].reshape(span, HD) for j in range(2)]
+        none = jnp.zeros_like(both[0])
+        queries = jnp.concatenate(
+            [jnp.concatenate([both[0], none], axis=1), jnp.concatenate([none, both[1]], axis=1)], axis=0
+        )
+        scores = [dot(k_ref[i * step:(i + 1) * step, lanes], queries, NT) for i in range(pieces)]
+        top = rounded(jnp.max(scores[0][:shift], axis=0, keepdims=True))
+        total = None
+        for i in range(pieces):
+            weights = jnp.exp2((scores[i] - top) * factor).astype(jnp.bfloat16)
+            values = v_ref[i * step:(i + 1) * step, lanes]
+            values = jnp.concatenate([values, jnp.ones((step, ROWS), jnp.bfloat16)], axis=1)
+            more = dot(values, weights, TN)
+            total = more if total is None else total + more
+        for j in range(2):
+            head, cols = pair * 2 + j, slice(j * span, (j + 1) * span)
+            outs = total[j * HD:(j + 1) * HD, cols].T.astype(jnp.bfloat16)
+            for dev in range(devices):
+                out_refs[0][dev * heads + head] = outs[dev * ROWS:(dev + 1) * ROWS]
+            top_ref[pl.ds(head, 1)] = top[:, cols]
+            sum_ref[pl.ds(head, 1)] = total[2 * HD:2 * HD + 1, cols]
+
     def head_part(head, pieces, shift):
         step = length // pieces
-        lanes = pl.ds(pl.multiple_of(head * HD, HD), HD)
+        lanes = slice(head * HD, (head + 1) * HD) if isinstance(head, int) else pl.ds(pl.multiple_of(head * HD, HD), HD)
         queries = jnp.concatenate([r[:, head].reshape(span, HD) for r in q_refs], axis=0)
         scores = [dot(k_ref[i * step:(i + 1) * step, lanes], queries, NT) for i in range(pieces)]
         top = rounded(jnp.max(scores[0][:shift], axis=0, keepdims=True))
@@ -81,14 +119,18 @@
             total = more if total is None else total + more
         outs = total[:HD].T.astype(jnp.bfloat16)
         for i in range(parts):
-            out_refs[i][:, head] = outs[i * span:(i + 1) * span].reshape(devices, ROWS, HD)
+            for dev in range(devices):
+                first = i * span + dev * ROWS
+                out_refs[i][dev * heads + head] = outs[first:first + ROWS]
         top_ref[pl.ds(head, 1)] = top
         sum_ref[pl.ds(head, 1)] = total[HD:HD + 1]
 
-    @pl.loop(0, heads // 4)
-    def _(i):
-        for j in range(4):
-            head_part(i * 4 + j, 4, 256)
+    if parts == 1:
+        for pair in range(heads // 2):
+            pair_part(pair, 8, 128)
+    else:
+        for head in range(heads):
+            head_part(head, 4, 64)
 
     @pl.when(jnp.logical_not(jnp.max(sum_ref[...]) < 2.0 ** 64))
     def _():
@@ -98,10 +140,10 @@
 
     for i in range(parts):
         part = slice(i * span, (i + 1) * span)
-        out_refs[i][:, heads] = stat_rows(by_device(top_ref[:, part]), by_device(sum_ref[:, part]))
-
-
-def prefix_part(after, queries, keys, values, factor):
+        write_packed_stats(out_refs[i], by_device(top_ref[:, part]), by_device(sum_ref[:, part]))
+
+
+def prefix_part(after, queries, keys, values, factor, cost=1.0):
     parts = len(queries)
     devices, heads = queries[0].shape[:2]
     length = keys.shape[0]
@@ -110,13 +152,13 @@
         functools.partial(prefix_kernel, factor, parts),
         in_specs=[pl.BlockSpec(memory_space=pl.ANY)] + [VMEM] * (parts + 2),
         out_specs=[VMEM] * parts,
-        out_shape=[jax.ShapeDtypeStruct((devices, heads + 1, ROWS, HD), jnp.bfloat16)] * parts,
+        out_shape=[jax.ShapeDtypeStruct((devices * heads + 2, ROWS, HD), jnp.bfloat16)] * parts,
         scratch_shapes=[pltpu.VMEM((heads, rows), jnp.float32)] * 2,
         compiler_params=pltpu.CompilerParams(vmem_limit_bytes=32 * 2**20),
         cost_estimate=pl.CostEstimate(
-            flops=8 * rows * heads * length * HD,
-            bytes_accessed=4 * length * heads * HD + 4 * rows * heads * HD,
-            transcendentals=rows * heads * length,
+            flops=int(cost * 8 * rows * heads * length * HD),
+            bytes_accessed=int(cost * 4 * (length + rows) * heads * HD),
+            transcendentals=int(cost * rows * heads * length),
         ),
         name="prefix_part",
     )(after, *queries, keys, values)
@@ -186,7 +228,7 @@
     part_refs, out_ref = refs[:-1], refs[-1]
     devices = out_ref.shape[0]
     heads = out_ref.shape[1] - 1
-    stats = [read_stats(r) for r in part_refs]
+    stats = [read_packed_stats(r) for r in part_refs]
     top = functools.reduce(jnp.maximum, [s[0] for s in stats])
     scales = [jnp.exp2((s[0] - top) * factor) for s in stats]
     out_ref[:, heads] = stat_rows(top, sum(f * s[1] for f, s in zip(scales, stats)))
@@ -194,7 +236,7 @@
     for dev in range(devices):
         acc = None
         for i, r in enumerate(part_refs):
-            block = r[dev, :heads].reshape(heads * ROWS, HD).astype(jnp.float32)
+            block = r[dev * heads:(dev + 1) * heads].reshape(heads * ROWS, HD).astype(jnp.float32)
             term = block * turned[:, i * devices + dev:i * devices + dev + 1]
             acc = term if acc is None else acc + term
         out_ref[dev, :heads] = acc.astype(jnp.bfloat16).reshape(heads, ROWS, HD)
@@ -205,7 +247,7 @@
         functools.partial(merge_kernel, factor),
         in_specs=[VMEM] * len(parts),
         out_specs=VMEM,
-        out_shape=jax.ShapeDtypeStruct(parts[0].shape, jnp.bfloat16),
+        out_shape=jax.ShapeDtypeStruct((Z, parts[0].shape[0] // Z + 1, ROWS, HD), jnp.bfloat16),
         compiler_params=pltpu.CompilerParams(vmem_limit_bytes=16 * 2**20),
         name="merge_part",
     )(*parts)
@@ -259,12 +301,12 @@
     suf_out, suf_stats = suffix_part(
         suffix_len, column, mine, suffix_keys, suffix_values, prefix_keys, prefix_values, factor
     )
-    column, before, after = lax.optimization_barrier((column, before, after))
-    across = shift_x(column, 2)
+    across = shift_x(before, 1)
     for_before, for_after = prefix_part(suf_stats, [before, after], prefix_keys, prefix_values, factor)
     from_after, from_before = shift_x(for_before, -1), shift_x(for_after, 1)
-    for_own, for_across = prefix_part(suf_stats, [column, across], prefix_keys, prefix_values, factor)
+    [for_across] = prefix_part(for_before, [across], prefix_keys, prefix_values, factor)
     from_across = shift_x(for_across, 2)
+    [for_own] = prefix_part(for_across, [column], prefix_keys, prefix_values, factor, cost=0.01)
     merged = merge_part([for_own, from_after, from_before, from_across], factor)
     got = swap_z(merged)
     out = combine_part(got, suf_out, suf_stats, factor)

time: 90.7 us -> 86.4 us (0.953)
  the two profiles are of different devices: /device:TPU:22 before, /device:TPU:12 now
where the time goes in v4:
time: 86.4 us; the launch traced here: 85.9 us
  blocking collectives  56.9 us (66%)
  Pallas kernels  15.6 us (18%)
  starting transfers between devices  6.72 us (8%)
  waiting for transfers between devices  5.85 us (7%)
    all_to_all x2, blocking collectives, swap_z(): lax.all_to_all(array, 'ctx', 0, 0, axis_index_groups=groups, tiled=True)  56.9 us
    pallas_call x3, Pallas kernels, prefix_part(): pl.pallas_call(functools.partial(prefix_kernel, factor, parts), in_specs=...  11.2 us
    ppermute x6, starting transfers between devices, shift_x(): return lax.ppermute(array, 'ctx', pairs)  6.72 us
    ppermute x6, waiting for transfers between devices, shift_x(): return lax.ppermute(array, 'ctx', pairs)  5.85 us
    pallas_call x1, Pallas kernels, suffix_part(): pl.pallas_call(functools.partial(suffix_kernel, factor), in_specs=[pl.Blo...  2.54 us
  transfers between devices with their start and end apart: 6, of which 2 were waited for; matrix products, arithmetic and copies ran while one was open for 0% of the time, Pallas kernels for 16%

profile of v4, /device:TPU:12, one launch (start us, length us, event | category | flops | bytes accessed | tf_op | source)
XLA Modules:
  0.0 85.9 jit_solution(10464087314381621847)
XLA Ops:
  0.0 0.8 copy-done.4
  0.8 0.0 copy-start.5
  0.8 0.0 copy-start.6
  0.8 20.4 %all_to_all.10.after_ref.refs_0_ = bf16[8,8,16,128]{3,2,1,0:T(8,128)(2,1)S(1)} all-to-all(bf16[8,8,16,128]{3,2,1,0:T(8,128)(2,1)S(1)} %spread_part.1), channel_id=1, replica_groups={{0,4,8,12,16,20,24,28},{1,5,9,13,17,21,25,29},{2,6,10,14,18,22,26,30},{..., dimensions={0} | all-to-all | bytes 524288 | tf_op jit(solution)/shard_map/all_to_all | solution.py:291
  21.2 1.2 %collective-permute-start = (bf16[8,8,16,128]{3,2,1,0:T(8,128)(2,1)S(1)}, bf16[8,8,16,128]{3,2,1,0:T(8,128)(2,1)S(1)}, u32[]{:S(2)}, u32[]{:S(2)}) collective-permute-start(bf16[8,8,16,128]{3,2,1,0:T(8,128)(2,1)S(1)} %all_to_all.10.after_ref.refs_0_), channel_id=1, source_target_pairs={{0,1},{1,2},{2,3},{3,0},{4,5},{5,6},{6,7},{7,4},{8,9},{9,10},{10,1... | collective-permute-start | bytes 786440 | tf_op jit(solution)/shard_map/ppermute | solution.py:286
  22.4 0.8 collective-permute-start.1
  23.3 0.0 copy-done.2
  23.3 2.5 %suffix_part.1 = (f32[128,128]{1,0:T(8,128)S(1)}, f32[8,128]{1,0:T(8,128)S(1)}) custom-call(s32[2]{0:T(128)S(1)} %copy-done.6, bf16[8,8,16,128]{3,2,1,0:T(8,128)(2,1)S(1)} %all_to_all.10.after_ref.refs_0_, bf16[8,16,128]{2,1,0:T(8,128)(2,1)S(1)} %bitcast.11, bf16[2,256,1024]{2,1,0:T(8,128)(2,1)S(1)} %copy-done.2, bf16[2,256,1024]{2,1,0:T(8,128)(2,1)S(1)} %copy-done.3, ...), custom_call_target="tpu_custom_call" | custom-call | flops 1073741824 | bytes 8388608 | tf_op jit(solution)/shard_map/suffix_part/pallas_call | solution.py:213
  25.8 2.2 %collective-permute-done.refs_0_ = bf16[8,8,16,128]{3,2,1,0:T(8,128)(2,1)S(1)} collective-permute-done((bf16[8,8,16,128]{3,2,1,0:T(8,128)(2,1)S(1)}, bf16[8,8,16,128]{3,2,1,0:T(8,128)(2,1)S(1)}, u32[]{:S(2)}, u32[]{:S(2)}) %collective-permute-start) | collective-permute-done | bytes 262176 | tf_op jit(solution)/shard_map/ppermute | solution.py:286
  28.0 1.2 %collective-permute-start.2 = (bf16[8,8,16,128]{3,2,1,0:T(8,128)(2,1)S(1)}, bf16[8,8,16,128]{3,2,1,0:T(8,128)(2,1)S(1)}, u32[]{:S(2)}, u32[]{:S(2)}) collective-permute-start(bf16[8,8,16,128]{3,2,1,0:T(8,128)(2,1)S(1)} %collective-permute-done.refs_0_), channel_id=1, source_target_pairs={{0,1},{1,2},{2,3},{3,0},{4,5},{5,6},{6,7},{7,4},{8,9},{9,10},{10,1... | collective-permute-start | bytes 786440 | tf_op jit(solution)/shard_map/ppermute | solution.py:286
  29.2 0.0 collective-permute-done.1.refs_1_
  29.2 4.7 %prefix_part.3 = (bf16[66,16,128]{2,1,0:T(8,128)(2,1)S(1)}, bf16[66,16,128]{2,1,0:T(8,128)(2,1)S(1)}) custom-call(f32[8,128]{1,0:T(8,128)S(1)} %get-tuple-element.9.after_ref.stat_ref, bf16[8,8,16,128]{3,2,1,0:T(8,128)(2,1)S(1)} %collective-permute-done.refs_0_, bf16[8,8,16,128]{3,2,1,0:T(8,128)(2,1)S(1)} %collective-permute-done.1.refs_1_, ...), custom_call_target="tpu_custom_call" | custom-call | flops 4294967296 | bytes 9437184 | tf_op jit(solution)/shard_map/prefix_part/pallas_call | solution.py:151
  34.0 0.9 %collective-permute-start.3 = (bf16[66,16,128]{2,1,0:T(8,128)(2,1)S(1)}, bf16[66,16,128]{2,1,0:T(8,128)(2,1)S(1)}, u32[]{:S(2)}, u32[]{:S(2)}) collective-permute-start(bf16[66,16,128]{2,1,0:T(8,128)(2,1)S(1)} %get-tuple-element.10.after_ref), channel_id=1, source_target_pairs={{0,3},{1,0},{2,1},{3,2},{4,7},{5,4},{6,5},{7,6},{8,11},{9,8},{10,9... | collective-permute-start | bytes 811016 | tf_op jit(solution)/shard_map/ppermute | solution.py:286
  34.9 1.2 %collective-permute-start.4 = (bf16[66,16,128]{2,1,0:T(8,128)(2,1)S(1)}, bf16[66,16,128]{2,1,0:T(8,128)(2,1)S(1)}, u32[]{:S(2)}, u32[]{:S(2)}) collective-permute-start(bf16[66,16,128]{2,1,0:T(8,128)(2,1)S(1)} %get-tuple-element.11), channel_id=1, source_target_pairs={{0,1},{1,2},{2,3},{3,0},{4,5},{5,6},{6,7},{7,4},{8,9},{9,10},{10,1... | collective-permute-start | bytes 811016 | tf_op jit(solution)/shard_map/ppermute | solution.py:286
  36.1 0.0 collective-permute-done.2.refs_0_
  36.1 3.2 %prefix_part.4.after_ref = bf16[66,16,128]{2,1,0:T(8,128)(2,1)S(1)} custom-call(bf16[66,16,128]{2,1,0:T(8,128)(2,1)S(1)} %get-tuple-element.10.after_ref, bf16[8,8,16,128]{3,2,1,0:T(8,128)(2,1)S(1)} %collective-permute-done.2.refs_0_, bf16[2048,1024]{1,0:T(8,128)(2,1)S(1)} %copy-done, bf16[2048,1024]{1,0:T(8,128)(2,1)S(1)} %copy-done.1), custom_call_target="tpu_custom_call" | custom-call | flops 2147483648 | bytes 8912896 | tf_op jit(solution)/shard_map/prefix_part/pallas_call | solution.py:151
  39.4 1.4 %collective-permute-start.5 = (bf16[66,16,128]{2,1,0:T(8,128)(2,1)S(1)}, bf16[66,16,128]{2,1,0:T(8,128)(2,1)S(1)}, u32[]{:S(2)}, u32[]{:S(2)}) collective-permute-start(bf16[66,16,128]{2,1,0:T(8,128)(2,1)S(1)} %prefix_part.4.after_ref), channel_id=1, source_target_pairs={{0,2},{1,3},{2,0},{3,1},{4,6},{5,7},{6,4},{7,5},{8,10},{9,11},{10,... | collective-permute-start | bytes 811016 | tf_op jit(solution)/shard_map/ppermute | solution.py:286
  40.7 3.2 %prefix_part.5.refs_0_ = bf16[66,16,128]{2,1,0:T(8,128)(2,1)S(1)} custom-call(bf16[66,16,128]{2,1,0:T(8,128)(2,1)S(1)} %prefix_part.4.after_ref, bf16[8,8,16,128]{3,2,1,0:T(8,128)(2,1)S(1)} %all_to_all.10.after_ref.refs_0_, bf16[2048,1024]{1,0:T(8,128)(2,1)S(1)} %copy-done, bf16[2048,1024]{1,0:T(8,128)(2,1)S(1)} %copy-done.1), custom_call_target="tpu_custom_call" | custom-call | flops 21474836 | bytes 89128 | tf_op jit(solution)/shard_map/prefix_part/pallas_call | solution.py:151
  44.0 0.0 collective-permute-done.3.refs_1_
  44.0 0.0 collective-permute-done.4.refs_2_
  44.0 3.6 %collective-permute-done.5.refs_3_ = bf16[66,16,128]{2,1,0:T(8,128)(2,1)S(1)} collective-permute-done((bf16[66,16,128]{2,1,0:T(8,128)(2,1)S(1)}, bf16[66,16,128]{2,1,0:T(8,128)(2,1)S(1)}, u32[]{:S(2)}, u32[]{:S(2)}) %collective-permute-start.5) | collective-permute-done | bytes 270368 | tf_op jit(solution)/shard_map/ppermute | solution.py:286
  47.6 0.8 merge_part.1
  48.4 36.5 %all_to_all.11.got_ref = bf16[8,9,16,128]{3,2,1,0:T(8,128)(2,1)S(1)} all-to-all(bf16[8,9,16,128]{3,2,1,0:T(8,128)(2,1)S(1)} %merge_part.1), channel_id=1, replica_groups={{0,4,8,12,16,20,24,28},{1,5,9,13,17,21,25,29},{2,6,10,14,18,22,26,30},{..., dimensions={0} | all-to-all | bytes 589824 | tf_op jit(solution)/shard_map/all_to_all | solution.py:291
  84.9 1.0 %combine_part.1 = bf16[128,128]{1,0:T(8,128)(2,1)} custom-call(bf16[8,9,16,128]{3,2,1,0:T(8,128)(2,1)S(1)} %all_to_all.11.got_ref, f32[128,128]{1,0:T(8,128)S(1)} %get-tuple-element.12.suf_ref, f32[8,128]{1,0:T(8,128)S(1)} %get-tuple-element.9.after_ref.stat_ref), custom_call_target="tpu_custom_call" | custom-call | tf_op jit(solution)/shard_map/combine_part/pallas_call | solution.py:274
  (11 shorter events, 0.1 us)
Async XLA Ops:
  0.0 0.8 copy-start.4
  0.8 22.5 %copy-start = (bf16[2048,1024]{1,0:T(8,128)(2,1)S(1)}, bf16[2048,1024]{1,0:T(8,128)(2,1)}, u32[]{:S(2)}) copy-start(bf16[2048,1024]{1,0:T(8,128)(2,1)} %refs_1_.3) | copy-start | bytes 12582916
  0.8 22.5 %copy-start.1 = (bf16[2048,1024]{1,0:T(8,128)(2,1)S(1)}, bf16[2048,1024]{1,0:T(8,128)(2,1)}, u32[]{:S(2)}) copy-start(bf16[2048,1024]{1,0:T(8,128)(2,1)} %refs_2_.5) | copy-start | bytes 12582916
  0.8 22.5 %copy-start.2 = (bf16[2,256,1024]{2,1,0:T(8,128)(2,1)S(1)}, bf16[2,256,1024]{2,1,0:T(8,128)(2,1)}, u32[]{:S(2)}) copy-start(bf16[2,256,1024]{2,1,0:T(8,128)(2,1)} %sk_ref.1) | copy-start | bytes 3145732
  0.8 22.5 %copy-start.3 = (bf16[2,256,1024]{2,1,0:T(8,128)(2,1)S(1)}, bf16[2,256,1024]{2,1,0:T(8,128)(2,1)}, u32[]{:S(2)}) copy-start(bf16[2,256,1024]{2,1,0:T(8,128)(2,1)} %sv_ref.1) | copy-start | bytes 3145732
  0.8 22.5 %copy-start.5 = (bf16[2,8192]{1,0:T(2,128)(2,1)S(1)}, bf16[2,8192]{1,0:T(2,128)(2,1)}, u32[]{:S(2)}) copy-start(bf16[2,8192]{1,0:T(2,128)(2,1)} %param.6) | copy-start | bytes 98308
  0.8 22.5 %copy-start.6 = (s32[2]{0:T(128)S(1)}, s32[2]{0:T(128)}, u32[]{:S(2)}) copy-start(s32[2]{0:T(128)} %len_ref.1) | copy-start | bytes 28
  21.2 6.8 %collective-permute-start = (bf16[8,8,16,128]{3,2,1,0:T(8,128)(2,1)S(1)}, bf16[8,8,16,128]{3,2,1,0:T(8,128)(2,1)S(1)}, u32[]{:S(2)}, u32[]{:S(2)}) collective-permute-start(bf16[8,8,16,128]{3,2,1,0:T(8,128)(2,1)S(1)} %all_to_all.10.after_ref.refs_0_), channel_id=1, source_target_pairs={{0,1},{1,2},{2,3},{3,0},{4,5},{5,6},{6,7},{7,4},{8,9},{9,10},{10,1... | collective-permute-start | bytes 786440 | tf_op jit(solution)/shard_map/ppermute | solution.py:286
  22.4 6.8 %collective-permute-start.1 = (bf16[8,8,16,128]{3,2,1,0:T(8,128)(2,1)S(1)}, bf16[8,8,16,128]{3,2,1,0:T(8,128)(2,1)S(1)}, u32[]{:S(2)}, u32[]{:S(2)}) collective-permute-start(bf16[8,8,16,128]{3,2,1,0:T(8,128)(2,1)S(1)} %all_to_all.10.after_ref.refs_0_), channel_id=1, source_target_pairs={{0,3},{1,0},{2,1},{3,2},{4,7},{5,4},{6,5},{7,6},{8,11},{9,8},{10,9... | collective-permute-start | bytes 786440 | tf_op jit(solution)/shard_map/ppermute | solution.py:286
  28.0 8.1 %collective-permute-start.2 = (bf16[8,8,16,128]{3,2,1,0:T(8,128)(2,1)S(1)}, bf16[8,8,16,128]{3,2,1,0:T(8,128)(2,1)S(1)}, u32[]{:S(2)}, u32[]{:S(2)}) collective-permute-start(bf16[8,8,16,128]{3,2,1,0:T(8,128)(2,1)S(1)} %collective-permute-done.refs_0_), channel_id=1, source_target_pairs={{0,1},{1,2},{2,3},{3,0},{4,5},{5,6},{6,7},{7,4},{8,9},{9,10},{10,1... | collective-permute-start | bytes 786440 | tf_op jit(solution)/shard_map/ppermute | solution.py:286
  34.0 10.0 %collective-permute-start.3 = (bf16[66,16,128]{2,1,0:T(8,128)(2,1)S(1)}, bf16[66,16,128]{2,1,0:T(8,128)(2,1)S(1)}, u32[]{:S(2)}, u32[]{:S(2)}) collective-permute-start(bf16[66,16,128]{2,1,0:T(8,128)(2,1)S(1)} %get-tuple-element.10.after_ref), channel_id=1, source_target_pairs={{0,3},{1,0},{2,1},{3,2},{4,7},{5,4},{6,5},{7,6},{8,11},{9,8},{10,9... | collective-permute-start | bytes 811016 | tf_op jit(solution)/shard_map/ppermute | solution.py:286
  34.9 9.1 %collective-permute-start.4 = (bf16[66,16,128]{2,1,0:T(8,128)(2,1)S(1)}, bf16[66,16,128]{2,1,0:T(8,128)(2,1)S(1)}, u32[]{:S(2)}, u32[]{:S(2)}) collective-permute-start(bf16[66,16,128]{2,1,0:T(8,128)(2,1)S(1)} %get-tuple-element.11), channel_id=1, source_target_pairs={{0,1},{1,2},{2,3},{3,0},{4,5},{5,6},{6,7},{7,4},{8,9},{9,10},{10,1... | collective-permute-start | bytes 811016 | tf_op jit(solution)/shard_map/ppermute | solution.py:286
  39.4 8.3 %collective-permute-start.5 = (bf16[66,16,128]{2,1,0:T(8,128)(2,1)S(1)}, bf16[66,16,128]{2,1,0:T(8,128)(2,1)S(1)}, u32[]{:S(2)}, u32[]{:S(2)}) collective-permute-start(bf16[66,16,128]{2,1,0:T(8,128)(2,1)S(1)} %prefix_part.4.after_ref), channel_id=1, source_target_pairs={{0,2},{1,3},{2,0},{3,1},{4,6},{5,7},{6,4},{7,5},{8,10},{9,11},{10,... | collective-permute-start | bytes 811016 | tf_op jit(solution)/shard_map/ppermute | solution.py:286

commit v5 on v4

--- a/solution.py
+++ b/solution.py
@@ -224,14 +224,15 @@
     )(lengths, after, queries, suffix_keys, suffix_values, keys, values)
 
 
-def merge_kernel(factor, *refs):
-    part_refs, out_ref = refs[:-1], refs[-1]
+def premerge_kernel(factor, *refs):
+    part_refs, (out_ref, top_ref, sum_ref) = refs[:-3], refs[-3:]
     devices = out_ref.shape[0]
-    heads = out_ref.shape[1] - 1
+    heads = out_ref.shape[1] // ROWS
     stats = [read_packed_stats(r) for r in part_refs]
     top = functools.reduce(jnp.maximum, [s[0] for s in stats])
     scales = [jnp.exp2((s[0] - top) * factor) for s in stats]
-    out_ref[:, heads] = stat_rows(top, sum(f * s[1] for f, s in zip(scales, stats)))
+    top_ref[...] = top
+    sum_ref[...] = sum(f * s[1] for f, s in zip(scales, stats))
     turned = columns(scales)
     for dev in range(devices):
         acc = None
@@ -239,18 +240,49 @@
             block = r[dev * heads:(dev + 1) * heads].reshape(heads * ROWS, HD).astype(jnp.float32)
             term = block * turned[:, i * devices + dev:i * devices + dev + 1]
             acc = term if acc is None else acc + term
+        out_ref[dev] = acc
+
+
+def premerge_part(parts, factor):
+    heads = parts[0].shape[0] // Z
+    return pl.pallas_call(
+        functools.partial(premerge_kernel, factor),
+        in_specs=[VMEM] * len(parts),
+        out_specs=[VMEM] * 3,
+        out_shape=[
+            jax.ShapeDtypeStruct((Z, heads * ROWS, HD), jnp.float32),
+            jax.ShapeDtypeStruct((Z, HD), jnp.float32),
+            jax.ShapeDtypeStruct((Z, HD), jnp.float32),
+        ],
+        compiler_params=pltpu.CompilerParams(vmem_limit_bytes=16 * 2**20),
+        name="premerge_part",
+    )(*parts)
+
+
+def merge_kernel(factor, acc_ref, acc_top_ref, acc_sum_ref, last_ref, out_ref):
+    devices = out_ref.shape[0]
+    heads = out_ref.shape[1] - 1
+    last_top, last_sum = read_packed_stats(last_ref)
+    top = jnp.maximum(acc_top_ref[...], last_top)
+    scales = [jnp.exp2((t - top) * factor) for t in (acc_top_ref[...], last_top)]
+    rows = stat_rows(top, scales[0] * acc_sum_ref[...] + scales[1] * last_sum)
+    turned = columns(scales)
+    for dev in range(devices):
+        block = last_ref[dev * heads:(dev + 1) * heads].reshape(heads * ROWS, HD).astype(jnp.float32)
+        acc = acc_ref[dev] * turned[:, dev:dev + 1] + block * turned[:, devices + dev:devices + dev + 1]
         out_ref[dev, :heads] = acc.astype(jnp.bfloat16).reshape(heads, ROWS, HD)
-
-
-def merge_part(parts, factor):
+        out_ref[dev, heads] = rows[dev]
+
+
+def merge_part(merged, last, factor):
     return pl.pallas_call(
         functools.partial(merge_kernel, factor),
-        in_specs=[VMEM] * len(parts),
+        in_specs=[VMEM] * (len(merged) + 1),
         out_specs=VMEM,
-        out_shape=jax.ShapeDtypeStruct((Z, parts[0].shape[0] // Z + 1, ROWS, HD), jnp.bfloat16),
+        out_shape=jax.ShapeDtypeStruct((Z, last.shape[0] // Z + 1, ROWS, HD), jnp.bfloat16),
         compiler_params=pltpu.CompilerParams(vmem_limit_bytes=16 * 2**20),
         name="merge_part",
-    )(*parts)
+    )(*merged, last)
 
 
 def combine_kernel(factor, got_ref, suf_ref, stat_ref, out_ref):
@@ -307,7 +339,8 @@
     [for_across] = prefix_part(for_before, [across], prefix_keys, prefix_values, factor)
     from_across = shift_x(for_across, 2)
     [for_own] = prefix_part(for_across, [column], prefix_keys, prefix_values, factor, cost=0.01)
-    merged = merge_part([for_own, from_after, from_before, from_across], factor)
+    early = premerge_part([for_own, from_after, from_before], factor)
+    merged = merge_part(early, from_across, factor)
     got = swap_z(merged)
     out = combine_part(got, suf_out, suf_stats, factor)
     return out.reshape(heads * 8, owned, HD).transpose(1, 0, 2).reshape(owned, width)

time: 86.4 us -> 87.1 us (level)
  the two profiles are of different devices: /device:TPU:12 before, /device:TPU:22 now
where the time goes in v5:
time: 87.1 us; the launch traced here: 86.6 us
  blocking collectives  56.5 us (65%)
  Pallas kernels  15.9 us (18%)
  starting transfers between devices  7.12 us (8%)
  waiting for transfers between devices  6.14 us (7%)
    all_to_all x2, blocking collectives, swap_z(): lax.all_to_all(array, 'ctx', 0, 0, axis_index_groups=groups, tiled=True)  56.5 us
    pallas_call x3, Pallas kernels, prefix_part(): pl.pallas_call(functools.partial(prefix_kernel, factor, parts), in_specs=...  11.2 us
    ppermute x6, starting transfers between devices, shift_x(): return lax.ppermute(array, 'ctx', pairs)  7.12 us
    ppermute x6, waiting for transfers between devices, shift_x(): return lax.ppermute(array, 'ctx', pairs)  6.14 us
    pallas_call x1, Pallas kernels, suffix_part(): pl.pallas_call(functools.partial(suffix_kernel, factor), in_specs=[pl.Blo...  2.54 us
  transfers between devices with their start and end apart: 6, of which 2 were waited for; matrix products, arithmetic and copies ran while one was open for 0% of the time, Pallas kernels for 17%

profile of v5, /device:TPU:22, one launch (start us, length us, event | category | flops | bytes accessed | tf_op | source)
XLA Modules:
  0.0 86.6 jit_solution(7903676804267121910)
XLA Ops:
  0.0 0.8 copy-done.4
  0.8 0.0 copy-start.5
  0.8 0.0 copy-start.6
  0.8 20.4 %all_to_all.10.after_ref.refs_0_ = bf16[8,8,16,128]{3,2,1,0:T(8,128)(2,1)S(1)} all-to-all(bf16[8,8,16,128]{3,2,1,0:T(8,128)(2,1)S(1)} %spread_part.1), channel_id=1, replica_groups={{0,4,8,12,16,20,24,28},{1,5,9,13,17,21,25,29},{2,6,10,14,18,22,26,30},{..., dimensions={0} | all-to-all | bytes 524288 | tf_op jit(solution)/shard_map/all_to_all | solution.py:323
  21.2 0.5 collective-permute-start
  21.7 1.5 %collective-permute-start.1 = (bf16[8,8,16,128]{3,2,1,0:T(8,128)(2,1)S(1)}, bf16[8,8,16,128]{3,2,1,0:T(8,128)(2,1)S(1)}, u32[]{:S(2)}, u32[]{:S(2)}) collective-permute-start(bf16[8,8,16,128]{3,2,1,0:T(8,128)(2,1)S(1)} %all_to_all.10.after_ref.refs_0_), channel_id=1, source_target_pairs={{0,3},{1,0},{2,1},{3,2},{4,7},{5,4},{6,5},{7,6},{8,11},{9,8},{10,9... | collective-permute-start | bytes 786440 | tf_op jit(solution)/shard_map/ppermute | solution.py:318
  23.3 2.5 %suffix_part.1 = (f32[128,128]{1,0:T(8,128)S(1)}, f32[8,128]{1,0:T(8,128)S(1)}) custom-call(s32[2]{0:T(128)S(1)} %copy-done.6, bf16[8,8,16,128]{3,2,1,0:T(8,128)(2,1)S(1)} %all_to_all.10.after_ref.refs_0_, bf16[8,16,128]{2,1,0:T(8,128)(2,1)S(1)} %bitcast.11, bf16[2,256,1024]{2,1,0:T(8,128)(2,1)S(1)} %copy-done.2, bf16[2,256,1024]{2,1,0:T(8,128)(2,1)S(1)} %copy-done.3, ...), custom_call_target="tpu_custom_call" | custom-call | flops 1073741824 | bytes 8388608 | tf_op jit(solution)/shard_map/suffix_part/pallas_call | solution.py:213
  25.8 2.2 %collective-permute-done.refs_0_ = bf16[8,8,16,128]{3,2,1,0:T(8,128)(2,1)S(1)} collective-permute-done((bf16[8,8,16,128]{3,2,1,0:T(8,128)(2,1)S(1)}, bf16[8,8,16,128]{3,2,1,0:T(8,128)(2,1)S(1)}, u32[]{:S(2)}, u32[]{:S(2)}) %collective-permute-start) | collective-permute-done | bytes 262176 | tf_op jit(solution)/shard_map/ppermute | solution.py:318
  28.0 1.2 %collective-permute-start.2 = (bf16[8,8,16,128]{3,2,1,0:T(8,128)(2,1)S(1)}, bf16[8,8,16,128]{3,2,1,0:T(8,128)(2,1)S(1)}, u32[]{:S(2)}, u32[]{:S(2)}) collective-permute-start(bf16[8,8,16,128]{3,2,1,0:T(8,128)(2,1)S(1)} %collective-permute-done.refs_0_), channel_id=1, source_target_pairs={{0,1},{1,2},{2,3},{3,0},{4,5},{5,6},{6,7},{7,4},{8,9},{9,10},{10,1... | collective-permute-start | bytes 786440 | tf_op jit(solution)/shard_map/ppermute | solution.py:318
  29.3 0.0 collective-permute-done.1.refs_1_
  29.3 4.7 %prefix_part.3 = (bf16[66,16,128]{2,1,0:T(8,128)(2,1)S(1)}, bf16[66,16,128]{2,1,0:T(8,128)(2,1)S(1)}) custom-call(f32[8,128]{1,0:T(8,128)S(1)} %get-tuple-element.12.after_ref.stat_ref, bf16[8,8,16,128]{3,2,1,0:T(8,128)(2,1)S(1)} %collective-permute-done.refs_0_, bf16[8,8,16,128]{3,2,1,0:T(8,128)(2,1)S(1)} %collective-permute-done.1.refs_1_, ...), custom_call_target="tpu_custom_call" | custom-call | flops 4294967296 | bytes 9437184 | tf_op jit(solution)/shard_map/prefix_part/pallas_call | solution.py:151
  34.0 0.8 collective-permute-start.4
  34.8 1.3 %collective-permute-start.3 = (bf16[66,16,128]{2,1,0:T(8,128)(2,1)S(1)}, bf16[66,16,128]{2,1,0:T(8,128)(2,1)S(1)}, u32[]{:S(2)}, u32[]{:S(2)}) collective-permute-start(bf16[66,16,128]{2,1,0:T(8,128)(2,1)S(1)} %get-tuple-element.13.after_ref), channel_id=1, source_target_pairs={{0,3},{1,0},{2,1},{3,2},{4,7},{5,4},{6,5},{7,6},{8,11},{9,8},{10,9... | collective-permute-start | bytes 811016 | tf_op jit(solution)/shard_map/ppermute | solution.py:318
  36.2 0.0 collective-permute-done.2.refs_0_
  36.2 3.2 %prefix_part.4.after_ref = bf16[66,16,128]{2,1,0:T(8,128)(2,1)S(1)} custom-call(bf16[66,16,128]{2,1,0:T(8,128)(2,1)S(1)} %get-tuple-element.13.after_ref, bf16[8,8,16,128]{3,2,1,0:T(8,128)(2,1)S(1)} %collective-permute-done.2.refs_0_, bf16[2048,1024]{1,0:T(8,128)(2,1)S(1)} %copy-done, bf16[2048,1024]{1,0:T(8,128)(2,1)S(1)} %copy-done.1), custom_call_target="tpu_custom_call" | custom-call | flops 2147483648 | bytes 8912896 | tf_op jit(solution)/shard_map/prefix_part/pallas_call | solution.py:151
  39.4 1.7 %collective-permute-start.5 = (bf16[66,16,128]{2,1,0:T(8,128)(2,1)S(1)}, bf16[66,16,128]{2,1,0:T(8,128)(2,1)S(1)}, u32[]{:S(2)}, u32[]{:S(2)}) collective-permute-start(bf16[66,16,128]{2,1,0:T(8,128)(2,1)S(1)} %prefix_part.4.after_ref), channel_id=1, source_target_pairs={{0,2},{1,3},{2,0},{3,1},{4,6},{5,7},{6,4},{7,5},{8,10},{9,11},{10,... | collective-permute-start | bytes 811016 | tf_op jit(solution)/shard_map/ppermute | solution.py:318
  41.1 3.2 %prefix_part.5.refs_0_ = bf16[66,16,128]{2,1,0:T(8,128)(2,1)S(1)} custom-call(bf16[66,16,128]{2,1,0:T(8,128)(2,1)S(1)} %prefix_part.4.after_ref, bf16[8,8,16,128]{3,2,1,0:T(8,128)(2,1)S(1)} %all_to_all.10.after_ref.refs_0_, bf16[2048,1024]{1,0:T(8,128)(2,1)S(1)} %copy-done, bf16[2048,1024]{1,0:T(8,128)(2,1)S(1)} %copy-done.1), custom_call_target="tpu_custom_call" | custom-call | flops 21474836 | bytes 89128 | tf_op jit(solution)/shard_map/prefix_part/pallas_call | solution.py:151
  44.4 0.0 collective-permute-done.4.refs_2_
  44.4 3.9 %collective-permute-done.3.refs_1_ = bf16[66,16,128]{2,1,0:T(8,128)(2,1)S(1)} collective-permute-done((bf16[66,16,128]{2,1,0:T(8,128)(2,1)S(1)}, bf16[66,16,128]{2,1,0:T(8,128)(2,1)S(1)}, u32[]{:S(2)}, u32[]{:S(2)}) %collective-permute-start.3) | collective-permute-done | bytes 270368 | tf_op jit(solution)/shard_map/ppermute | solution.py:318
  48.3 0.6 premerge_part.1
  49.0 0.0 collective-permute-done.5.last_ref
  49.0 0.5 merge_part.1
  49.5 36.1 %all_to_all.11.got_ref = bf16[8,9,16,128]{3,2,1,0:T(8,128)(2,1)S(1)} all-to-all(bf16[8,9,16,128]{3,2,1,0:T(8,128)(2,1)S(1)} %merge_part.1), channel_id=1, replica_groups={{0,4,8,12,16,20,24,28},{1,5,9,13,17,21,25,29},{2,6,10,14,18,22,26,30},{..., dimensions={0} | all-to-all | bytes 589824 | tf_op jit(solution)/shard_map/all_to_all | solution.py:323
  85.6 1.0 %combine_part.1 = bf16[128,128]{1,0:T(8,128)(2,1)} custom-call(bf16[8,9,16,128]{3,2,1,0:T(8,128)(2,1)S(1)} %all_to_all.11.got_ref, f32[128,128]{1,0:T(8,128)S(1)} %get-tuple-element.18.suf_ref, f32[8,128]{1,0:T(8,128)S(1)} %get-tuple-element.12.after_ref.stat_ref), custom_call_target="tpu_custom_call" | custom-call | tf_op jit(solution)/shard_map/combine_part/pallas_call | solution.py:306
  (12 shorter events, 0.1 us)
Async XLA Ops:
  0.0 0.8 copy-start.4
  0.8 22.5 %copy-start = (bf16[2048,1024]{1,0:T(8,128)(2,1)S(1)}, bf16[2048,1024]{1,0:T(8,128)(2,1)}, u32[]{:S(2)}) copy-start(bf16[2048,1024]{1,0:T(8,128)(2,1)} %refs_1_.3) | copy-start | bytes 12582916
  0.8 22.5 %copy-start.1 = (bf16[2048,1024]{1,0:T(8,128)(2,1)S(1)}, bf16[2048,1024]{1,0:T(8,128)(2,1)}, u32[]{:S(2)}) copy-start(bf16[2048,1024]{1,0:T(8,128)(2,1)} %refs_2_.5) | copy-start | bytes 12582916
  0.8 22.5 %copy-start.2 = (bf16[2,256,1024]{2,1,0:T(8,128)(2,1)S(1)}, bf16[2,256,1024]{2,1,0:T(8,128)(2,1)}, u32[]{:S(2)}) copy-start(bf16[2,256,1024]{2,1,0:T(8,128)(2,1)} %sk_ref.1) | copy-start | bytes 3145732
  0.8 22.5 %copy-start.3 = (bf16[2,256,1024]{2,1,0:T(8,128)(2,1)S(1)}, bf16[2,256,1024]{2,1,0:T(8,128)(2,1)}, u32[]{:S(2)}) copy-start(bf16[2,256,1024]{2,1,0:T(8,128)(2,1)} %sv_ref.1) | copy-start | bytes 3145732
  0.8 22.5 %copy-start.5 = (bf16[2,8192]{1,0:T(2,128)(2,1)S(1)}, bf16[2,8192]{1,0:T(2,128)(2,1)}, u32[]{:S(2)}) copy-start(bf16[2,8192]{1,0:T(2,128)(2,1)} %param.6) | copy-start | bytes 98308
  0.8 22.5 %copy-start.6 = (s32[2]{0:T(128)S(1)}, s32[2]{0:T(128)}, u32[]{:S(2)}) copy-start(s32[2]{0:T(128)} %len_ref.1) | copy-start | bytes 28
  21.2 6.8 %collective-permute-start = (bf16[8,8,16,128]{3,2,1,0:T(8,128)(2,1)S(1)}, bf16[8,8,16,128]{3,2,1,0:T(8,128)(2,1)S(1)}, u32[]{:S(2)}, u32[]{:S(2)}) collective-permute-start(bf16[8,8,16,128]{3,2,1,0:T(8,128)(2,1)S(1)} %all_to_all.10.after_ref.refs_0_), channel_id=1, source_target_pairs={{0,1},{1,2},{2,3},{3,0},{4,5},{5,6},{6,7},{7,4},{8,9},{9,10},{10,1... | collective-permute-start | bytes 786440 | tf_op jit(solution)/shard_map/ppermute | solution.py:318
  21.7 7.6 %collective-permute-start.1 = (bf16[8,8,16,128]{3,2,1,0:T(8,128)(2,1)S(1)}, bf16[8,8,16,128]{3,2,1,0:T(8,128)(2,1)S(1)}, u32[]{:S(2)}, u32[]{:S(2)}) collective-permute-start(bf16[8,8,16,128]{3,2,1,0:T(8,128)(2,1)S(1)} %all_to_all.10.after_ref.refs_0_), channel_id=1, source_target_pairs={{0,3},{1,0},{2,1},{3,2},{4,7},{5,4},{6,5},{7,6},{8,11},{9,8},{10,9... | collective-permute-start | bytes 786440 | tf_op jit(solution)/shard_map/ppermute | solution.py:318
  28.0 8.1 %collective-permute-start.2 = (bf16[8,8,16,128]{3,2,1,0:T(8,128)(2,1)S(1)}, bf16[8,8,16,128]{3,2,1,0:T(8,128)(2,1)S(1)}, u32[]{:S(2)}, u32[]{:S(2)}) collective-permute-start(bf16[8,8,16,128]{3,2,1,0:T(8,128)(2,1)S(1)} %collective-permute-done.refs_0_), channel_id=1, source_target_pairs={{0,1},{1,2},{2,3},{3,0},{4,5},{5,6},{6,7},{7,4},{8,9},{9,10},{10,1... | collective-permute-start | bytes 786440 | tf_op jit(solution)/shard_map/ppermute | solution.py:318
  34.0 10.3 %collective-permute-start.4 = (bf16[66,16,128]{2,1,0:T(8,128)(2,1)S(1)}, bf16[66,16,128]{2,1,0:T(8,128)(2,1)S(1)}, u32[]{:S(2)}, u32[]{:S(2)}) collective-permute-start(bf16[66,16,128]{2,1,0:T(8,128)(2,1)S(1)} %get-tuple-element.14), channel_id=1, source_target_pairs={{0,1},{1,2},{2,3},{3,0},{4,5},{5,6},{6,7},{7,4},{8,9},{9,10},{10,1... | collective-permute-start | bytes 811016 | tf_op jit(solution)/shard_map/ppermute | solution.py:318
  34.8 13.5 %collective-permute-start.3 = (bf16[66,16,128]{2,1,0:T(8,128)(2,1)S(1)}, bf16[66,16,128]{2,1,0:T(8,128)(2,1)S(1)}, u32[]{:S(2)}, u32[]{:S(2)}) collective-permute-start(bf16[66,16,128]{2,1,0:T(8,128)(2,1)S(1)} %get-tuple-element.13.after_ref), channel_id=1, source_target_pairs={{0,3},{1,0},{2,1},{3,2},{4,7},{5,4},{6,5},{7,6},{8,11},{9,8},{10,9... | collective-permute-start | bytes 811016 | tf_op jit(solution)/shard_map/ppermute | solution.py:318
  39.4 9.6 %collective-permute-start.5 = (bf16[66,16,128]{2,1,0:T(8,128)(2,1)S(1)}, bf16[66,16,128]{2,1,0:T(8,128)(2,1)S(1)}, u32[]{:S(2)}, u32[]{:S(2)}) collective-permute-start(bf16[66,16,128]{2,1,0:T(8,128)(2,1)S(1)} %prefix_part.4.after_ref), channel_id=1, source_target_pairs={{0,2},{1,3},{2,0},{3,1},{4,6},{5,7},{6,4},{7,5},{8,10},{9,11},{10,... | collective-permute-start | bytes 811016 | tf_op jit(solution)/shard_map/ppermute | solution.py:318

commit v6 on v5

--- a/solution.py
+++ b/solution.py
@@ -130,7 +130,7 @@
             pair_part(pair, 8, 128)
     else:
         for head in range(heads):
-            head_part(head, 4, 64)
+            head_part(head, 4, 16)
 
     @pl.when(jnp.logical_not(jnp.max(sum_ref[...]) < 2.0 ** 64))
     def _():

time: 87.1 us -> 86.6 us (level)
  the two profiles are of different devices: /device:TPU:22 before, /device:TPU:32 now
where the time goes in v6:
time: 86.6 us; the launch traced here: 85.4 us
  blocking collectives  53.9 us (62%)
  Pallas kernels  15.8 us (18%)
  starting transfers between devices  9.94 us (11%)
  waiting for transfers between devices  4.93 us (6%)
    all_to_all x2, blocking collectives, swap_z(): lax.all_to_all(array, 'ctx', 0, 0, axis_index_groups=groups, tiled=True)  53.9 us
    pallas_call x3, Pallas kernels, prefix_part(): pl.pallas_call(functools.partial(prefix_kernel, factor, parts), in_specs=...  11.1 us
    ppermute x6, starting transfers between devices, shift_x(): return lax.ppermute(array, 'ctx', pairs)  9.94 us
    ppermute x6, waiting for transfers between devices, shift_x(): return lax.ppermute(array, 'ctx', pairs)  4.93 us
    pallas_call x1, Pallas kernels, suffix_part(): pl.pallas_call(functools.partial(suffix_kernel, factor), in_specs=[pl.Blo...  2.54 us
  transfers between devices with their start and end apart: 6, of which 3 were waited for; matrix products, arithmetic and copies ran while one was open for 0% of the time, Pallas kernels for 17%

profile of v6, /device:TPU:32, one launch (start us, length us, event | category | flops | bytes accessed | tf_op | source)
XLA Modules:
  0.0 85.4 jit_solution(7703866287545150673)
XLA Ops:
  0.0 0.8 copy-done.4
  0.8 0.0 copy-start.5
  0.8 19.0 %all_to_all.10.after_ref.refs_0_ = bf16[8,8,16,128]{3,2,1,0:T(8,128)(2,1)S(1)} all-to-all(bf16[8,8,16,128]{3,2,1,0:T(8,128)(2,1)S(1)} %spread_part.1), channel_id=1, replica_groups={{0,4,8,12,16,20,24,28},{1,5,9,13,17,21,25,29},{2,6,10,14,18,22,26,30},{..., dimensions={0} | all-to-all | bytes 524288 | tf_op jit(solution)/shard_map/all_to_all | solution.py:323
  19.9 1.5 %collective-permute-start = (bf16[8,8,16,128]{3,2,1,0:T(8,128)(2,1)S(1)}, bf16[8,8,16,128]{3,2,1,0:T(8,128)(2,1)S(1)}, u32[]{:S(2)}, u32[]{:S(2)}) collective-permute-start(bf16[8,8,16,128]{3,2,1,0:T(8,128)(2,1)S(1)} %all_to_all.10.after_ref.refs_0_), channel_id=1, source_target_pairs={{0,1},{1,2},{2,3},{3,0},{4,5},{5,6},{6,7},{7,4},{8,9},{9,10},{10,1... | collective-permute-start | bytes 786440 | tf_op jit(solution)/shard_map/ppermute | solution.py:318
  21.4 1.7 %collective-permute-start.1 = (bf16[8,8,16,128]{3,2,1,0:T(8,128)(2,1)S(1)}, bf16[8,8,16,128]{3,2,1,0:T(8,128)(2,1)S(1)}, u32[]{:S(2)}, u32[]{:S(2)}) collective-permute-start(bf16[8,8,16,128]{3,2,1,0:T(8,128)(2,1)S(1)} %all_to_all.10.after_ref.refs_0_), channel_id=1, source_target_pairs={{0,3},{1,0},{2,1},{3,2},{4,7},{5,4},{6,5},{7,6},{8,11},{9,8},{10,9... | collective-permute-start | bytes 786440 | tf_op jit(solution)/shard_map/ppermute | solution.py:318
  23.1 0.0 copy-done.1
  23.2 2.5 %suffix_part.1 = (f32[128,128]{1,0:T(8,128)S(1)}, f32[8,128]{1,0:T(8,128)S(1)}) custom-call(s32[2]{0:T(128)S(1)} %copy-done.6, bf16[8,8,16,128]{3,2,1,0:T(8,128)(2,1)S(1)} %all_to_all.10.after_ref.refs_0_, bf16[8,16,128]{2,1,0:T(8,128)(2,1)S(1)} %bitcast.11, bf16[2,256,1024]{2,1,0:T(8,128)(2,1)S(1)} %copy-done.2, bf16[2,256,1024]{2,1,0:T(8,128)(2,1)S(1)} %copy-done.3, ...), custom_call_target="tpu_custom_call" | custom-call | flops 1073741824 | bytes 8388608 | tf_op jit(solution)/shard_map/suffix_part/pallas_call | solution.py:213
  25.7 1.8 %collective-permute-done.refs_0_ = bf16[8,8,16,128]{3,2,1,0:T(8,128)(2,1)S(1)} collective-permute-done((bf16[8,8,16,128]{3,2,1,0:T(8,128)(2,1)S(1)}, bf16[8,8,16,128]{3,2,1,0:T(8,128)(2,1)S(1)}, u32[]{:S(2)}, u32[]{:S(2)}) %collective-permute-start) | collective-permute-done | bytes 262176 | tf_op jit(solution)/shard_map/ppermute | solution.py:318
  27.5 1.5 %collective-permute-start.2 = (bf16[8,8,16,128]{3,2,1,0:T(8,128)(2,1)S(1)}, bf16[8,8,16,128]{3,2,1,0:T(8,128)(2,1)S(1)}, u32[]{:S(2)}, u32[]{:S(2)}) collective-permute-start(bf16[8,8,16,128]{3,2,1,0:T(8,128)(2,1)S(1)} %collective-permute-done.refs_0_), channel_id=1, source_target_pairs={{0,1},{1,2},{2,3},{3,0},{4,5},{5,6},{6,7},{7,4},{8,9},{9,10},{10,1... | collective-permute-start | bytes 786440 | tf_op jit(solution)/shard_map/ppermute | solution.py:318
  29.0 0.0 collective-permute-done.1.refs_1_
  29.0 4.6 %prefix_part.3 = (bf16[66,16,128]{2,1,0:T(8,128)(2,1)S(1)}, bf16[66,16,128]{2,1,0:T(8,128)(2,1)S(1)}) custom-call(f32[8,128]{1,0:T(8,128)S(1)} %get-tuple-element.12.after_ref.stat_ref, bf16[8,8,16,128]{3,2,1,0:T(8,128)(2,1)S(1)} %collective-permute-done.refs_0_, bf16[8,8,16,128]{3,2,1,0:T(8,128)(2,1)S(1)} %collective-permute-done.1.refs_1_, ...), custom_call_target="tpu_custom_call" | custom-call | flops 4294967296 | bytes 9437184 | tf_op jit(solution)/shard_map/prefix_part/pallas_call | solution.py:151
  33.6 1.6 %collective-permute-start.4 = (bf16[66,16,128]{2,1,0:T(8,128)(2,1)S(1)}, bf16[66,16,128]{2,1,0:T(8,128)(2,1)S(1)}, u32[]{:S(2)}, u32[]{:S(2)}) collective-permute-start(bf16[66,16,128]{2,1,0:T(8,128)(2,1)S(1)} %get-tuple-element.14), channel_id=1, source_target_pairs={{0,1},{1,2},{2,3},{3,0},{4,5},{5,6},{6,7},{7,4},{8,9},{9,10},{10,1... | collective-permute-start | bytes 811016 | tf_op jit(solution)/shard_map/ppermute | solution.py:318
  35.2 1.7 %collective-permute-start.3 = (bf16[66,16,128]{2,1,0:T(8,128)(2,1)S(1)}, bf16[66,16,128]{2,1,0:T(8,128)(2,1)S(1)}, u32[]{:S(2)}, u32[]{:S(2)}) collective-permute-start(bf16[66,16,128]{2,1,0:T(8,128)(2,1)S(1)} %get-tuple-element.13.after_ref), channel_id=1, source_target_pairs={{0,3},{1,0},{2,1},{3,2},{4,7},{5,4},{6,5},{7,6},{8,11},{9,8},{10,9... | collective-permute-start | bytes 811016 | tf_op jit(solution)/shard_map/ppermute | solution.py:318
  37.0 0.9 %collective-permute-done.2.refs_0_ = bf16[8,8,16,128]{3,2,1,0:T(8,128)(2,1)S(1)} collective-permute-done((bf16[8,8,16,128]{3,2,1,0:T(8,128)(2,1)S(1)}, bf16[8,8,16,128]{3,2,1,0:T(8,128)(2,1)S(1)}, u32[]{:S(2)}, u32[]{:S(2)}) %collective-permute-start.2) | collective-permute-done | bytes 262176 | tf_op jit(solution)/shard_map/ppermute | solution.py:318
  37.8 3.2 %prefix_part.4.after_ref = bf16[66,16,128]{2,1,0:T(8,128)(2,1)S(1)} custom-call(bf16[66,16,128]{2,1,0:T(8,128)(2,1)S(1)} %get-tuple-element.13.after_ref, bf16[8,8,16,128]{3,2,1,0:T(8,128)(2,1)S(1)} %collective-permute-done.2.refs_0_, bf16[2048,1024]{1,0:T(8,128)(2,1)S(1)} %copy-done, bf16[2048,1024]{1,0:T(8,128)(2,1)S(1)} %copy-done.1), custom_call_target="tpu_custom_call" | custom-call | flops 2147483648 | bytes 8912896 | tf_op jit(solution)/shard_map/prefix_part/pallas_call | solution.py:151
  41.1 1.9 %collective-permute-start.5 = (bf16[66,16,128]{2,1,0:T(8,128)(2,1)S(1)}, bf16[66,16,128]{2,1,0:T(8,128)(2,1)S(1)}, u32[]{:S(2)}, u32[]{:S(2)}) collective-permute-start(bf16[66,16,128]{2,1,0:T(8,128)(2,1)S(1)} %prefix_part.4.after_ref), channel_id=1, source_target_pairs={{0,2},{1,3},{2,0},{3,1},{4,6},{5,7},{6,4},{7,5},{8,10},{9,11},{10,... | collective-permute-start | bytes 811016 | tf_op jit(solution)/shard_map/ppermute | solution.py:318
  43.0 3.2 %prefix_part.5.refs_0_ = bf16[66,16,128]{2,1,0:T(8,128)(2,1)S(1)} custom-call(bf16[66,16,128]{2,1,0:T(8,128)(2,1)S(1)} %prefix_part.4.after_ref, bf16[8,8,16,128]{3,2,1,0:T(8,128)(2,1)S(1)} %all_to_all.10.after_ref.refs_0_, bf16[2048,1024]{1,0:T(8,128)(2,1)S(1)} %copy-done, bf16[2048,1024]{1,0:T(8,128)(2,1)S(1)} %copy-done.1), custom_call_target="tpu_custom_call" | custom-call | flops 21474836 | bytes 89128 | tf_op jit(solution)/shard_map/prefix_part/pallas_call | solution.py:151
  46.2 0.0 collective-permute-done.4.refs_2_
  46.2 0.0 collective-permute-done.3.refs_1_
  46.2 0.6 premerge_part.1
  46.9 2.3 %collective-permute-done.5.last_ref = bf16[66,16,128]{2,1,0:T(8,128)(2,1)S(1)} collective-permute-done((bf16[66,16,128]{2,1,0:T(8,128)(2,1)S(1)}, bf16[66,16,128]{2,1,0:T(8,128)(2,1)S(1)}, u32[]{:S(2)}, u32[]{:S(2)}) %collective-permute-start.5) | collective-permute-done | bytes 270368 | tf_op jit(solution)/shard_map/ppermute | solution.py:318
  49.1 0.5 merge_part.1
  49.6 34.8 %all_to_all.11.got_ref = bf16[8,9,16,128]{3,2,1,0:T(8,128)(2,1)S(1)} all-to-all(bf16[8,9,16,128]{3,2,1,0:T(8,128)(2,1)S(1)} %merge_part.1), channel_id=1, replica_groups={{0,4,8,12,16,20,24,28},{1,5,9,13,17,21,25,29},{2,6,10,14,18,22,26,30},{..., dimensions={0} | all-to-all | bytes 589824 | tf_op jit(solution)/shard_map/all_to_all | solution.py:323
  84.4 1.0 %combine_part.1 = bf16[128,128]{1,0:T(8,128)(2,1)} custom-call(bf16[8,9,16,128]{3,2,1,0:T(8,128)(2,1)S(1)} %all_to_all.11.got_ref, f32[128,128]{1,0:T(8,128)S(1)} %get-tuple-element.18.suf_ref, f32[8,128]{1,0:T(8,128)S(1)} %get-tuple-element.12.after_ref.stat_ref), custom_call_target="tpu_custom_call" | custom-call | tf_op jit(solution)/shard_map/combine_part/pallas_call | solution.py:306
  (12 shorter events, 0.1 us)
Async XLA Ops:
  0.0 0.8 copy-start.4
  0.8 22.4 %copy-start = (bf16[2048,1024]{1,0:T(8,128)(2,1)S(1)}, bf16[2048,1024]{1,0:T(8,128)(2,1)}, u32[]{:S(2)}) copy-start(bf16[2048,1024]{1,0:T(8,128)(2,1)} %refs_1_.3) | copy-start | bytes 12582916
  0.8 22.4 %copy-start.1 = (bf16[2048,1024]{1,0:T(8,128)(2,1)S(1)}, bf16[2048,1024]{1,0:T(8,128)(2,1)}, u32[]{:S(2)}) copy-start(bf16[2048,1024]{1,0:T(8,128)(2,1)} %refs_2_.5) | copy-start | bytes 12582916
  0.8 22.4 %copy-start.2 = (bf16[2,256,1024]{2,1,0:T(8,128)(2,1)S(1)}, bf16[2,256,1024]{2,1,0:T(8,128)(2,1)}, u32[]{:S(2)}) copy-start(bf16[2,256,1024]{2,1,0:T(8,128)(2,1)} %sk_ref.1) | copy-start | bytes 3145732
  0.8 22.4 %copy-start.3 = (bf16[2,256,1024]{2,1,0:T(8,128)(2,1)S(1)}, bf16[2,256,1024]{2,1,0:T(8,128)(2,1)}, u32[]{:S(2)}) copy-start(bf16[2,256,1024]{2,1,0:T(8,128)(2,1)} %sv_ref.1) | copy-start | bytes 3145732
  0.8 22.4 %copy-start.5 = (bf16[2,8192]{1,0:T(2,128)(2,1)S(1)}, bf16[2,8192]{1,0:T(2,128)(2,1)}, u32[]{:S(2)}) copy-start(bf16[2,8192]{1,0:T(2,128)(2,1)} %param.6) | copy-start | bytes 98308
  0.8 22.4 %copy-start.6 = (s32[2]{0:T(128)S(1)}, s32[2]{0:T(128)}, u32[]{:S(2)}) copy-start(s32[2]{0:T(128)} %len_ref.1) | copy-start | bytes 28
  19.9 7.6 %collective-permute-start = (bf16[8,8,16,128]{3,2,1,0:T(8,128)(2,1)S(1)}, bf16[8,8,16,128]{3,2,1,0:T(8,128)(2,1)S(1)}, u32[]{:S(2)}, u32[]{:S(2)}) collective-permute-start(bf16[8,8,16,128]{3,2,1,0:T(8,128)(2,1)S(1)} %all_to_all.10.after_ref.refs_0_), channel_id=1, source_target_pairs={{0,1},{1,2},{2,3},{3,0},{4,5},{5,6},{6,7},{7,4},{8,9},{9,10},{10,1... | collective-permute-start | bytes 786440 | tf_op jit(solution)/shard_map/ppermute | solution.py:318
  21.4 7.6 %collective-permute-start.1 = (bf16[8,8,16,128]{3,2,1,0:T(8,128)(2,1)S(1)}, bf16[8,8,16,128]{3,2,1,0:T(8,128)(2,1)S(1)}, u32[]{:S(2)}, u32[]{:S(2)}) collective-permute-start(bf16[8,8,16,128]{3,2,1,0:T(8,128)(2,1)S(1)} %all_to_all.10.after_ref.refs_0_), channel_id=1, source_target_pairs={{0,3},{1,0},{2,1},{3,2},{4,7},{5,4},{6,5},{7,6},{8,11},{9,8},{10,9... | collective-permute-start | bytes 786440 | tf_op jit(solution)/shard_map/ppermute | solution.py:318
  27.5 10.3 %collective-permute-start.2 = (bf16[8,8,16,128]{3,2,1,0:T(8,128)(2,1)S(1)}, bf16[8,8,16,128]{3,2,1,0:T(8,128)(2,1)S(1)}, u32[]{:S(2)}, u32[]{:S(2)}) collective-permute-start(bf16[8,8,16,128]{3,2,1,0:T(8,128)(2,1)S(1)} %collective-permute-done.refs_0_), channel_id=1, source_target_pairs={{0,1},{1,2},{2,3},{3,0},{4,5},{5,6},{6,7},{7,4},{8,9},{9,10},{10,1... | collective-permute-start | bytes 786440 | tf_op jit(solution)/shard_map/ppermute | solution.py:318
  33.6 12.6 %collective-permute-start.4 = (bf16[66,16,128]{2,1,0:T(8,128)(2,1)S(1)}, bf16[66,16,128]{2,1,0:T(8,128)(2,1)S(1)}, u32[]{:S(2)}, u32[]{:S(2)}) collective-permute-start(bf16[66,16,128]{2,1,0:T(8,128)(2,1)S(1)} %get-tuple-element.14), channel_id=1, source_target_pairs={{0,1},{1,2},{2,3},{3,0},{4,5},{5,6},{6,7},{7,4},{8,9},{9,10},{10,1... | collective-permute-start | bytes 811016 | tf_op jit(solution)/shard_map/ppermute | solution.py:318
  35.2 11.0 %collective-permute-start.3 = (bf16[66,16,128]{2,1,0:T(8,128)(2,1)S(1)}, bf16[66,16,128]{2,1,0:T(8,128)(2,1)S(1)}, u32[]{:S(2)}, u32[]{:S(2)}) collective-permute-start(bf16[66,16,128]{2,1,0:T(8,128)(2,1)S(1)} %get-tuple-element.13.after_ref), channel_id=1, source_target_pairs={{0,3},{1,0},{2,1},{3,2},{4,7},{5,4},{6,5},{7,6},{8,11},{9,8},{10,9... | collective-permute-start | bytes 811016 | tf_op jit(solution)/shard_map/ppermute | solution.py:318
  41.1 8.1 %collective-permute-start.5 = (bf16[66,16,128]{2,1,0:T(8,128)(2,1)S(1)}, bf16[66,16,128]{2,1,0:T(8,128)(2,1)S(1)}, u32[]{:S(2)}, u32[]{:S(2)}) collective-permute-start(bf16[66,16,128]{2,1,0:T(8,128)(2,1)S(1)} %prefix_part.4.after_ref), channel_id=1, source_target_pairs={{0,2},{1,3},{2,0},{3,1},{4,6},{5,7},{6,4},{7,5},{8,10},{9,11},{10,... | collective-permute-start | bytes 811016 | tf_op jit(solution)/shard_map/ppermute | solution.py:318
